TPU v7x, 512 devices: a whole 4x8x8 slice. The times are simulated.
512 devices in a mesh: gx: 8 (over y), gy: 16 (over z, core), gz: 4 (over x).
Axes of the slice: x: 4, y: 8, z: 8, core: 2. Of those that a mesh axis runs over, the one named last changes fastest.
Arguments:
- positions: float32 [8, 16, 4, 3, 1024], P('gx', 'gy', 'gz'), may hold values from 0 to 21.7, as said below
- polar: float32 [8, 16, 4, 1024], P('gx', 'gy', 'gz'), may hold values from 0.4 to 3
- field: float32 [8, 16, 4, 3, 1024], P('gx', 'gy', 'gz'), may hold values from -24 to 24
- groups: int32 [8, 16, 4, 1024], P('gx', 'gy', 'gz'), may hold values from 0 to 255, never falling along the last dimension, each value on 1 to 8 neighbouring positions
- pair_tiles: int32 [8, 16, 4, 3, 112], P('gx', 'gy', 'gz'), may hold values from 0 to 14, as said below
Outputs:
- dipoles: float32 [8, 16, 4, 3, 1024], P('gx', 'gy', 'gz')
- residual: float32 [8, 16, 4, 3, 1024], P('gx', 'gy', 'gz')
Inputs may be any that keep to these rules, and one draw needn't show every extreme that they name: `positions`: atom k of tile t of a device lies in the sub-box (t // 4, t // 2 % 2, t % 2) of edge 10.85 of the device's block, near a lattice site of that sub-box; two atoms are never closer than 0.6. `pair_tiles`: rows 0 and 2 hold tile numbers; row 1 holds the neighbour code (0 to 13, see the steps) of the device that holds the second tile, or 14 for an empty slot; empty slots come after all listed entries. With code 0 the first tile is at most the second. Every pair of occupied tiles whose sub-boxes touch (faces, edges or corners, periodically) is listed exactly once, by the device for which the other device's offset is one of the 14 codes. At most 112 entries are listed on one device, and some device lists 112.
All inputs are finite; a program needn't handle non-finite values.
Results may differ from a plain program's by a relative error of at most 0.0003.
Values sent between devices are 32-bit elements; how exact they have to be, the bound alone decides.
A program may use at most 64 MiB of HBM per device.

v0:
```python
import jax
import jax.numpy as jnp
from jax import lax
from jax.sharding import PartitionSpec as P

TILE = 128
ITERS = 2


THOLE_A = 0.39
BOX_EDGE = 21.7
CUT_ON = 7.0
CUT_OFF = 9.0
block_pairs = 8
shell_offsets = [
    (0, 0, 0),
    (0, 0, 1),
    (0, 1, -1),
    (0, 1, 0),
    (0, 1, 1),
    (1, -1, -1),
    (1, -1, 0),
    (1, -1, 1),
    (1, 0, -1),
    (1, 0, 0),
    (1, 0, 1),
    (1, 1, -1),
    (1, 1, 0),
    (1, 1, 1),
]


def with_halo(cells, sides, width):
    for axis, dim in sides:
        count = lax.axis_size(axis)
        head = lax.slice_in_dim(cells, 0, width, axis=dim)
        tail = lax.slice_in_dim(cells, cells.shape[dim] - width, cells.shape[dim], axis=dim)
        cells = jnp.concatenate(
            [
                lax.ppermute(tail, axis, [(i, (i + 1) % count) for i in range(count)]),
                cells,
                lax.ppermute(head, axis, [((i + 1) % count, i) for i in range(count)]),
            ],
            axis=dim,
        )
    return cells


def from_behind(array, axis, by):
    length = lax.axis_size(axis)
    return lax.ppermute(array, axis, [(i, (i + by) % length) for i in range(length)])


def coupling(first_pos, first_pol, second_pos, second_pol, offset, keep_mask):
    separation = second_pos[:, :, None, :] + offset[:, :, None, None] - first_pos[:, :, :, None]
    dist_sq = jnp.sum(separation * separation, axis=0) + jnp.where(keep_mask > 0, 0.0, 1.0)
    distance = jnp.sqrt(dist_sq)
    damping = (first_pol[:, :, None] * second_pol[:, None, :]) ** (1.0 / 6.0)
    damp_arg = THOLE_A * (distance / damping) ** 3
    screen_three = -jnp.expm1(-damp_arg)
    screen_five = screen_three - damp_arg * jnp.exp(-damp_arg)
    switch_arg = jnp.clip((distance - CUT_ON) / (CUT_OFF - CUT_ON), 0.0, 1.0)
    switch_val = 1.0 - switch_arg**3 * (10.0 - 15.0 * switch_arg + 6.0 * switch_arg * switch_arg)
    inv_cube = keep_mask * switch_val / (dist_sq * distance)
    return (separation, screen_three * inv_cube, 3.0 * screen_five * inv_cube / dist_sq)


def field_first(separation, coef_three, coef_five, second_dip):
    along = jnp.sum(separation * second_dip[:, :, None, :], axis=0)
    return jnp.sum(coef_five * along * separation - coef_three * second_dip[:, :, None, :], axis=-1)


def field_second(separation, coef_three, coef_five, first_dip):
    along = jnp.sum(separation * first_dip[:, :, :, None], axis=0)
    return jnp.sum(coef_five * along * separation - coef_three * first_dip[:, :, :, None], axis=-2)


def pair_keep(first_tile, near_code, second_tile, group_tile):
    listed = near_code < 14
    same_device = near_code == 0
    differ = group_tile[first_tile][:, :, None] != group_tile[second_tile][:, None, :]
    allowed = jnp.logical_and(
        listed[:, None, None], jnp.logical_or(jnp.logical_not(same_device)[:, None, None], differ)
    )
    weight = jnp.where(jnp.logical_and(same_device, first_tile == second_tile), 0.5, 1.0)
    return allowed.astype(jnp.float32) * weight[:, None, None]


def pair_offsets(near_code):
    clamped = jnp.minimum(near_code, 13)
    table = jnp.array(shell_offsets, jnp.float32).T
    return BOX_EDGE * table[:, clamped]


def slot_table():
    return jnp.array([ex * 9 + (ey + 1) * 3 + (ez + 1) for ex, ey, ez in shell_offsets], jnp.int32)


def gather_near(block_data):
    along_z = with_halo(block_data[None], (("gz", 0),), 1)
    along_y = with_halo(along_z[None], (("gy", 0),), 1)
    stacked = jnp.stack([along_y, from_behind(along_y, "gx", -1)])
    return stacked.reshape((18,) + block_data.shape)


def fold_back(far_field):
    folded = far_field.reshape((2, 3, 3) + far_field.shape[1:])
    folded = folded[0] + from_behind(folded[1], "gx", 1)
    folded = folded[1] + from_behind(folded[2], "gy", 1) + from_behind(folded[0], "gy", -1)
    return folded[1] + from_behind(folded[2], "gz", 1) + from_behind(folded[0], "gz", -1)


def block_count(listed):
    return (listed + block_pairs - 1) // block_pairs


def residual_sum(residual, precond):
    return lax.psum(jnp.sum(residual * precond), ("gx", "gy", "gz"))


def shards(positions, polar, field, groups, pair_tiles):
    tiles = positions.shape[-1] // TILE
    atom_data = jnp.concatenate([positions[0, 0, 0], polar[0, 0, 0][None]], axis=0).reshape(
        4, tiles, TILE
    )
    polar_tile = polar[0, 0, 0].reshape(1, tiles, TILE)
    group_tile = groups[0, 0, 0].reshape(tiles, TILE)
    field_init = field[0, 0, 0].reshape(3, tiles, TILE)
    slot_count = pair_tiles.shape[-1]
    padded = -(-slot_count // block_pairs) * block_pairs
    filler = jnp.broadcast_to(jnp.array([[0], [14], [0]], jnp.int32), (3, padded - slot_count))
    pair_list = jnp.concatenate([pair_tiles[0, 0, 0], filler], axis=1)
    listed_count = jnp.sum((pair_list[1] < 14).astype(jnp.int32))
    near_atoms = gather_near(atom_data)
    slot_of_code = slot_table()

    def apply_coupling(dipole_field):
        near_dip = gather_near(dipole_field)

        def one_block(block_number, totals):
            own_field, far_field = totals
            entries = lax.dynamic_slice_in_dim(
                pair_list, block_number * block_pairs, block_pairs, 1
            )
            first_tile, near_code, second_tile = (entries[0], entries[1], entries[2])
            grid_slot = slot_of_code[jnp.minimum(near_code, 13)]
            second_data = jnp.transpose(near_atoms[grid_slot, :, second_tile], (1, 0, 2))
            keep_mask = pair_keep(first_tile, near_code, second_tile, group_tile)
            separation, coef_three, coef_five = coupling(
                atom_data[:3][:, first_tile],
                atom_data[3][first_tile],
                second_data[:3],
                second_data[3],
                pair_offsets(near_code),
                keep_mask,
            )
            second_dip = jnp.transpose(near_dip[grid_slot, :, second_tile], (1, 0, 2))
            own_field = own_field.at[:, first_tile].add(
                field_first(separation, coef_three, coef_five, second_dip)
            )
            on_second = field_second(separation, coef_three, coef_five, dipole_field[:, first_tile])
            far_field = far_field.at[grid_slot, :, second_tile].add(
                jnp.transpose(on_second, (1, 0, 2))
            )
            return (own_field, far_field)

        start_fields = (
            jnp.zeros((3, tiles, TILE), jnp.float32),
            jnp.zeros((18, 3, tiles, TILE), jnp.float32),
        )
        own_field, far_field = lax.fori_loop(0, block_count(listed_count), one_block, start_fields)
        return own_field + fold_back(far_field)

    dipoles = polar_tile * field_init
    residual = apply_coupling(dipoles)
    precond = polar_tile * residual
    search = precond
    precond_dot = residual_sum(residual, precond)
    for iteration in range(ITERS):
        applied = search / polar_tile - apply_coupling(search)
        descent = precond_dot / lax.psum(jnp.sum(search * applied), ("gx", "gy", "gz"))
        dipoles = dipoles + descent * search
        residual = residual - descent * applied
        if iteration + 1 < ITERS:
            precond = polar_tile * residual
            next_dot = residual_sum(residual, precond)
            search = precond + next_dot / precond_dot * search
            precond_dot = next_dot
    atoms_here = tiles * TILE
    return (dipoles.reshape(1, 1, 1, 3, atoms_here), residual.reshape(1, 1, 1, 3, atoms_here))


def solution(mesh):
    placed = (
        P("gx", "gy", "gz", None, None),
        P("gx", "gy", "gz", None),
        P("gx", "gy", "gz", None, None),
        P("gx", "gy", "gz", None),
        P("gx", "gy", "gz", None, None),
    )
    return jax.shard_map(
        shards,
        mesh=mesh,
        in_specs=placed,
        out_specs=(P("gx", "gy", "gz", None, None), P("gx", "gy", "gz", None, None)),
        check_vma=False,
    )
```

profile of v0, /device:TPU:1, one launch (start us, length us, event | category | flops | bytes accessed | tf_op | source)
XLA Modules:
  0.0 913.5 jit_solution(12594644940853242426)
XLA Ops:
  1.3 3.9 collective-permute-start.5
  5.3 3.2 collective-permute-start.6
  12.0 4.4 collective-permute-start.1
  17.9 4.0 collective-permute-start.7
  21.9 3.4 collective-permute-start.8
  26.0 2.9 collective-permute-start.3
  29.0 4.2 collective-permute-start.9
  33.3 3.0 collective-permute-start.4
  40.1 125.4 %while.48 = (s32[]{:T(128)}, f32[3,8,128]{2,0,1:T(4,128)S(1)}, f32[18,3,8,128]{3,1,2,0:T(4,128)S(1)}, s32[]{:T(128)}, s32[3,112]{1,0:T(4,128)S(1)}, /*index=5*/f...) while((s32[]{:T(128)}, f32[3,8,128]{2,0,1:T(4,128)S(1)}, ...), condition=%wide.region_9.10_spmd.clone, body=%wide.region_1.9_spmd.sunk.clone.sunk | while | flops 10754310 | bytes 7919559 | solution.py:171
  167.6 4.8 collective-permute-done.10
  172.4 27.6 %collective-permute-start.12 = (f32[3,3,8,128]{3,2,1,0:T(8,128)S(1)}, f32[3,3,8,128]{3,2,1,0:T(8,128)S(1)}, u32[]{:S(2)}, u32[]{:S(2)}) collective-permute-start(f32[3,3,8,128]{3,2,1,0:T(8,128)S(1)} %get-tuple-element.944), channel_id=1, source_target_pairs={{0,60},{4,0},{8,4},{12,8},{16,12},{20,16},{24,20},{28,24},{32,28},... | collective-permute-start | bytes 110600 | tf_op jit(solution)/shard_map/ppermute | solution.py:51
  200.9 12.1 %collective-permute-start.13 = (f32[3,8,128]{2,1,0:T(8,128)S(1)}, f32[3,8,128]{2,1,0:T(8,128)S(1)}, u32[]{:S(2)}, u32[]{:S(2)}) collective-permute-start(f32[3,8,128]{2,1,0:T(8,128)S(1)} %get-tuple-element.949), channel_id=1, source_target_pairs={{0,1},{1,2},{2,3},{3,0},{4,5},{5,6},{6,7},{7,4},{8,9},{9,10},{10,1... | collective-permute-start | bytes 36872 | tf_op jit(solution)/shard_map/ppermute | solution.py:51
  214.9 2.5 collective-permute-done.14
  219.4 4.6 collective-permute-start.16
  226.0 5.1 collective-permute-start.18
  231.9 3.0 collective-permute-start.19
  237.6 125.4 %while.49 = (s32[]{:T(128)}, f32[3,8,128]{2,0,1:T(4,128)S(1)}, f32[18,3,8,128]{3,1,2,0:T(4,128)S(1)}, s32[]{:T(128)}, s32[3,112]{1,0:T(4,128)S(1)}, /*index=5*/f...) while((s32[]{:T(128)}, f32[3,8,128]{2,0,1:T(4,128)S(1)}, ...), condition=%wide.region_20.21_spmd.clone, body=%wide.region_12.20_spmd.sunk.clone.sunk | while | flops 10754310 | bytes 7919559 | solution.py:171
  365.1 4.8 collective-permute-done.20
  369.9 28.9 %collective-permute-start.22 = (f32[3,3,8,128]{3,2,1,0:T(8,128)S(1)}, f32[3,3,8,128]{3,2,1,0:T(8,128)S(1)}, u32[]{:S(2)}, u32[]{:S(2)}) collective-permute-start(f32[3,3,8,128]{3,2,1,0:T(8,128)S(1)} %get-tuple-element.940), channel_id=1, source_target_pairs={{0,60},{4,0},{8,4},{12,8},{16,12},{20,16},{24,20},{28,24},{32,28},... | collective-permute-start | bytes 110600 | tf_op jit(solution)/shard_map/ppermute | solution.py:51
  399.6 12.7 %collective-permute-start.23 = (f32[3,8,128]{2,1,0:T(8,128)S(1)}, f32[3,8,128]{2,1,0:T(8,128)S(1)}, u32[]{:S(2)}, u32[]{:S(2)}) collective-permute-start(f32[3,8,128]{2,1,0:T(8,128)S(1)} %get-tuple-element.947), channel_id=1, source_target_pairs={{0,1},{1,2},{2,3},{3,0},{4,5},{5,6},{6,7},{7,4},{8,9},{9,10},{10,1... | collective-permute-start | bytes 36872 | tf_op jit(solution)/shard_map/ppermute | solution.py:51
  417.5 99.5 %all-reduce = (f32[]{:T(128)}, f32[]{:T(128)}) all-reduce(f32[]{:T(128)} %get-tuple-element.822, f32[]{:T(128)} %get-tuple-element.821), channel_id=1, replica_groups=mesh['gx'=8,'gy'=16,'gz'=4] {'gx','gy','gz'}, use_global_device_ids=true, to_apply=%region_11.12 | all-reduce | flops 2 | bytes 16 | tf_op jit(solution)/shard_map/psum | solution.py:118
  518.8 94.7 %psum.30 = f32[]{:T(128)} all-reduce(f32[]{:T(128)} %get-tuple-element.893), channel_id=1, replica_groups=mesh['gx'=8,'gy'=16,'gz'=4] {'gx','gy','gz'}, use_global_device_ids=true, to_apply=%region_24.25 | all-reduce | flops 1 | bytes 8 | tf_op jit(solution)/shard_map/psum | solution.py:118
  614.8 3.1 collective-permute-start.25
  617.9 3.4 collective-permute-start.26
  622.4 2.7 collective-permute-start.27
  626.1 2.5 collective-permute-done.28
  631.1 3.7 collective-permute-done.29
  635.0 125.6 %while.50 = (s32[]{:T(128)}, f32[3,8,128]{2,0,1:T(4,128)S(1)}, f32[18,3,8,128]{3,1,2,0:T(4,128)S(1)}, s32[]{:T(128)}, s32[3,112]{1,0:T(4,128)S(1)}, /*index=5*/f...) while((s32[]{:T(128)}, f32[3,8,128]{2,0,1:T(4,128)S(1)}, ...), condition=%wide.region_33.34_spmd.clone, body=%wide.region_25.33_spmd.sunk.clone.sunk | while | flops 10754310 | bytes 7919559 | solution.py:171
  762.6 4.8 collective-permute-done.30
  767.5 25.2 %collective-permute-start.32 = (f32[3,3,8,128]{3,2,1,0:T(8,128)S(1)}, f32[3,3,8,128]{3,2,1,0:T(8,128)S(1)}, u32[]{:S(2)}, u32[]{:S(2)}) collective-permute-start(f32[3,3,8,128]{3,2,1,0:T(8,128)S(1)} %get-tuple-element.936), channel_id=1, source_target_pairs={{0,60},{4,0},{8,4},{12,8},{16,12},{20,16},{24,20},{28,24},{32,28},... | collective-permute-start | bytes 110600 | tf_op jit(solution)/shard_map/ppermute | solution.py:51
  793.6 14.9 %collective-permute-start.33 = (f32[3,8,128]{2,1,0:T(8,128)S(1)}, f32[3,8,128]{2,1,0:T(8,128)S(1)}, u32[]{:S(2)}, u32[]{:S(2)}) collective-permute-start(f32[3,8,128]{2,1,0:T(8,128)S(1)} %get-tuple-element.945), channel_id=1, source_target_pairs={{0,1},{1,2},{2,3},{3,0},{4,5},{5,6},{6,7},{7,4},{8,9},{9,10},{10,1... | collective-permute-start | bytes 36872 | tf_op jit(solution)/shard_map/ppermute | solution.py:51
  813.6 98.0 %psum.31 = f32[]{:T(128)} all-reduce(f32[]{:T(128)} %get-tuple-element.891), channel_id=1, replica_groups=mesh['gx'=8,'gy'=16,'gz'=4] {'gx','gy','gz'}, use_global_device_ids=true, to_apply=%region_35.36 | all-reduce | flops 1 | bytes 8 | tf_op jit(solution)/shard_map/psum | solution.py:181
  (1203 shorter events, 414.5 us)
Async XLA Ops:
  1.3 16.5 %collective-permute-start.5 = (f32[1,3,8,128]{3,1,2,0:T(4,128)S(1)}, f32[1,3,8,128]{3,1,2,0:T(4,128)S(1)}, u32[]{:S(2)}, u32[]{:S(2)}) collective-permute-start(f32[1,3,8,128]{3,1,2,0:T(4,128)S(1)} %copy_multiply_fusion), channel_id=1, source_target_pairs={{0,1},{1,2},{2,3},{3,0},{4,5},{5,6},{6,7},{7,4},{8,9},{9,10},{10,1... | collective-permute-start | bytes 36872 | tf_op jit(solution)/shard_map/ppermute | solution.py:40
  5.3 12.6 %collective-permute-start.6 = (f32[1,3,8,128]{3,1,2,0:T(4,128)S(1)}, f32[1,3,8,128]{3,1,2,0:T(4,128)S(1)}, u32[]{:S(2)}, u32[]{:S(2)}) collective-permute-start(f32[1,3,8,128]{3,1,2,0:T(4,128)S(1)} %copy_multiply_fusion), channel_id=1, source_target_pairs={{1,0},{2,1},{3,2},{0,3},{5,4},{6,5},{7,6},{4,7},{9,8},{10,9},{11,1... | collective-permute-start | bytes 36872 | tf_op jit(solution)/shard_map/ppermute | solution.py:42
  9.9 15.4 %collective-permute-start = (f32[1,4,8,128]{3,1,2,0:T(4,128)S(1)}, f32[1,4,8,128]{3,1,2,0:T(4,128)S(1)}, u32[]{:S(2)}, u32[]{:S(2)}) collective-permute-start(f32[1,4,8,128]{3,1,2,0:T(4,128)S(1)} %pad_maximum_fusion.8), channel_id=1, source_target_pairs={{0,1},{1,2},{2,3},{3,0},{4,5},{5,6},{6,7},{7,4},{8,9},{9,10},{10,1... | collective-permute-start | bytes 49160 | tf_op jit(solution)/shard_map/ppermute | solution.py:40
  12.0 13.3 %collective-permute-start.1 = (f32[1,4,8,128]{3,1,2,0:T(4,128)S(1)}, f32[1,4,8,128]{3,1,2,0:T(4,128)S(1)}, u32[]{:S(2)}, u32[]{:S(2)}) collective-permute-start(f32[1,4,8,128]{3,1,2,0:T(4,128)S(1)} %pad_maximum_fusion.8), channel_id=1, source_target_pairs={{1,0},{2,1},{3,2},{0,3},{5,4},{6,5},{7,6},{4,7},{9,8},{10,9},{11,1... | collective-permute-start | bytes 49160 | tf_op jit(solution)/shard_map/ppermute | solution.py:42
  17.9 11.1 %collective-permute-start.7 = (f32[1,3,3,8,128]{4,2,3,1,0:T(4,128)S(1)}, f32[1,3,3,8,128]{4,2,3,1,0:T(4,128)S(1)}, u32[]{:S(2)}, u32[]{:S(2)}) collective-permute-start(f32[1,3,3,8,128]{4,2,3,1,0:T(4,128)S(1)} %maximum_bitcast_fusion.1), channel_id=1, source_target_pairs={{0,4},{4,8},{8,12},{12,16},{16,20},{20,24},{24,28},{28,32},{32,36}... | collective-permute-start | bytes 110600 | tf_op jit(solution)/shard_map/ppermute | solution.py:40
  21.9 7.1 collective-permute-start.8
  26.0 7.2 collective-permute-start.2
  26.0 7.2 collective-permute-start.3
  29.0 8.6 collective-permute-start.9
  33.3 6.6 collective-permute-start.4
  165.6 6.7 collective-permute-start.10
  172.3 28.3 %collective-permute-start.11 = (f32[3,3,8,128]{3,2,1,0:T(8,128)S(1)}, f32[3,3,8,128]{3,2,1,0:T(8,128)S(1)}, u32[]{:S(2)}, u32[]{:S(2)}) collective-permute-start(f32[3,3,8,128]{3,2,1,0:T(8,128)S(1)} %get-tuple-element.943), channel_id=1, source_target_pairs={{0,4},{4,8},{8,12},{12,16},{16,20},{20,24},{24,28},{28,32},{32,36}... | collective-permute-start | bytes 110600 | tf_op jit(solution)/shard_map/ppermute | solution.py:51
  172.4 28.5 %collective-permute-start.12 = (f32[3,3,8,128]{3,2,1,0:T(8,128)S(1)}, f32[3,3,8,128]{3,2,1,0:T(8,128)S(1)}, u32[]{:S(2)}, u32[]{:S(2)}) collective-permute-start(f32[3,3,8,128]{3,2,1,0:T(8,128)S(1)} %get-tuple-element.944), channel_id=1, source_target_pairs={{0,60},{4,0},{8,4},{12,8},{16,12},{20,16},{24,20},{28,24},{32,28},... | collective-permute-start | bytes 110600 | tf_op jit(solution)/shard_map/ppermute | solution.py:51
  200.9 14.0 %collective-permute-start.13 = (f32[3,8,128]{2,1,0:T(8,128)S(1)}, f32[3,8,128]{2,1,0:T(8,128)S(1)}, u32[]{:S(2)}, u32[]{:S(2)}) collective-permute-start(f32[3,8,128]{2,1,0:T(8,128)S(1)} %get-tuple-element.949), channel_id=1, source_target_pairs={{0,1},{1,2},{2,3},{3,0},{4,5},{5,6},{6,7},{7,4},{8,9},{9,10},{10,1... | collective-permute-start | bytes 36872 | tf_op jit(solution)/shard_map/ppermute | solution.py:51
  213.0 4.4 collective-permute-start.14
  217.4 6.5 collective-permute-start.15
  219.4 5.4 collective-permute-start.16
  224.8 7.0 collective-permute-start.17
  226.0 5.9 collective-permute-start.18
  231.9 5.5 collective-permute-start.19
  363.1 6.7 collective-permute-start.20
  369.9 29.6 %collective-permute-start.21 = (f32[3,3,8,128]{3,2,1,0:T(8,128)S(1)}, f32[3,3,8,128]{3,2,1,0:T(8,128)S(1)}, u32[]{:S(2)}, u32[]{:S(2)}) collective-permute-start(f32[3,3,8,128]{3,2,1,0:T(8,128)S(1)} %get-tuple-element.939), channel_id=1, source_target_pairs={{0,4},{4,8},{8,12},{12,16},{16,20},{20,24},{24,28},{28,32},{32,36}... | collective-permute-start | bytes 110600 | tf_op jit(solution)/shard_map/ppermute | solution.py:51
  369.9 29.7 %collective-permute-start.22 = (f32[3,3,8,128]{3,2,1,0:T(8,128)S(1)}, f32[3,3,8,128]{3,2,1,0:T(8,128)S(1)}, u32[]{:S(2)}, u32[]{:S(2)}) collective-permute-start(f32[3,3,8,128]{3,2,1,0:T(8,128)S(1)} %get-tuple-element.940), channel_id=1, source_target_pairs={{0,60},{4,0},{8,4},{12,8},{16,12},{20,16},{24,20},{28,24},{32,28},... | collective-permute-start | bytes 110600 | tf_op jit(solution)/shard_map/ppermute | solution.py:51
  399.6 14.7 %collective-permute-start.23 = (f32[3,8,128]{2,1,0:T(8,128)S(1)}, f32[3,8,128]{2,1,0:T(8,128)S(1)}, u32[]{:S(2)}, u32[]{:S(2)}) collective-permute-start(f32[3,8,128]{2,1,0:T(8,128)S(1)} %get-tuple-element.947), channel_id=1, source_target_pairs={{0,1},{1,2},{2,3},{3,0},{4,5},{5,6},{6,7},{7,4},{8,9},{9,10},{10,1... | collective-permute-start | bytes 36872 | tf_op jit(solution)/shard_map/ppermute | solution.py:51
  412.4 4.4 collective-permute-start.24
  614.8 6.5 collective-permute-start.25
  617.9 4.4 collective-permute-start.26
  628.7 6.1 collective-permute-start.29
  760.7 6.7 collective-permute-start.30
  767.4 25.9 %collective-permute-start.31 = (f32[3,3,8,128]{3,2,1,0:T(8,128)S(1)}, f32[3,3,8,128]{3,2,1,0:T(8,128)S(1)}, u32[]{:S(2)}, u32[]{:S(2)}) collective-permute-start(f32[3,3,8,128]{3,2,1,0:T(8,128)S(1)} %get-tuple-element.935), channel_id=1, source_target_pairs={{0,4},{4,8},{8,12},{12,16},{16,20},{20,24},{24,28},{28,32},{32,36}... | collective-permute-start | bytes 110600 | tf_op jit(solution)/shard_map/ppermute | solution.py:51
  767.5 26.1 %collective-permute-start.32 = (f32[3,3,8,128]{3,2,1,0:T(8,128)S(1)}, f32[3,3,8,128]{3,2,1,0:T(8,128)S(1)}, u32[]{:S(2)}, u32[]{:S(2)}) collective-permute-start(f32[3,3,8,128]{3,2,1,0:T(8,128)S(1)} %get-tuple-element.936), channel_id=1, source_target_pairs={{0,60},{4,0},{8,4},{12,8},{16,12},{20,16},{24,20},{28,24},{32,28},... | collective-permute-start | bytes 110600 | tf_op jit(solution)/shard_map/ppermute | solution.py:51
  793.6 16.9 %collective-permute-start.33 = (f32[3,8,128]{2,1,0:T(8,128)S(1)}, f32[3,8,128]{2,1,0:T(8,128)S(1)}, u32[]{:S(2)}, u32[]{:S(2)}) collective-permute-start(f32[3,8,128]{2,1,0:T(8,128)S(1)} %get-tuple-element.945), channel_id=1, source_target_pairs={{0,1},{1,2},{2,3},{3,0},{4,5},{5,6},{6,7},{7,4},{8,9},{9,10},{10,1... | collective-permute-start | bytes 36872 | tf_op jit(solution)/shard_map/ppermute | solution.py:51
  (9 other events, 241.2 us)
where the time goes:
time: 915 us; the launch traced here: 914 us
  blocking collectives  292 us (32%)
  other arithmetic  202 us (22%)
  starting transfers between devices  192 us (21%)
  local copies, waits for them, and re-layouts  177 us (19%)
  waiting for transfers between devices  39 us (4%)
    psum x2, blocking collectives, residual_sum(): return lax.psum(jnp.sum(residual * precond), ('gx', 'gy', 'gz'))  194 us
    ppermute x19, starting transfers between devices, from_behind(): lax.ppermute(array, axis, [(i, (i + by) % length) for i in range(length)])  146 us
    psum x1, blocking collectives, shards(): lax.psum(jnp.sum(search * applied), ('gx', 'gy', 'gz'))  98 us
    reduce_sum x33, other arithmetic, field_second(): jnp.sum(coef_five * along * separation - coef_three * first_dip[:, :, :,...  50.9 us
    mul x33, other arithmetic, field_first(): coef_five * along * separation - coef_three * second_dip[:, :, None, :]  47.6 us
    reduce_sum x33, other arithmetic, field_second(): along = jnp.sum(separation * first_dip[:, :, :, None], axis=0)  36.1 us
    ppermute x19, waiting for transfers between devices, from_behind(): lax.ppermute(array, axis, [(i, (i + by) % length) for i in range(length)])  32.7 us
    scatter-add x33, other arithmetic, one_block(): far_field.at[grid_slot, :, second_tile]  28 us
  transfers between devices with their start and end apart: 35, of which 21 were waited for; matrix products, arithmetic and copies ran while one was open for 0% of the time, Pallas kernels for 0%

commit v1 on v0

v1 whole, which is shorter than its diff:
```python
import functools

import jax
import jax.numpy as jnp
import numpy as np
from jax import lax
from jax.experimental import pallas as pl
from jax.experimental.pallas import tpu as pltpu
from jax.sharding import PartitionSpec as P

TILE = 128
TILES = 8
AXES = ("gx", "gy", "gz")
BOX_EDGE = 21.7
THOLE_A = 0.39
FAR = 1000.0
MESH = pl.DeviceIdType.MESH
SHELL = [
    (0, 0, 0), (0, 0, 1), (0, 1, -1), (0, 1, 0), (0, 1, 1), (1, -1, -1), (1, -1, 0),
    (1, -1, 1), (1, 0, -1), (1, 0, 0), (1, 0, 1), (1, 1, -1), (1, 1, 0), (1, 1, 1),
]
N_SLOTS = 28
FACE, EDGE, CORNER, OWN, SELF = 0, 48, 72, 76, 104
ENTRIES = 112


def face_first(f, p):
    s = 1 + f + f * (f - 1) // 2
    return p // s * (2 * s) + s + p % s


def edge_first(k, p):
    g, sg = k // 2, k % 2
    free = 4 - 2 * g + g * (g - 1) // 2
    return free * p + 4 - 2 * ((2 - g) // 2) + (1 + g // 2) * sg


def corner_first(k):
    return 4 + k


def tables():
    messages, slot_tile, keys = [], [], []
    for f in range(3):
        s = 1 << f
        e = [0, 0, 0]
        e[2 - f] = 1
        messages.append((tuple(e), len(slot_tile), 4))
        slot_tile += [q // s * 2 * s + q % s for q in range(4)]
    for k in range(6):
        g, sg = k // 2, k % 2
        e = [[0, 1, 2 * sg - 1], [1, 0, 2 * sg - 1], [1, 2 * sg - 1, 0]][g]
        free, low = (4, 2, 1)[g], (1, 1, 2)[g]
        messages.append((tuple(e), len(slot_tile), 2))
        slot_tile += [free * q + low * (1 - sg) for q in range(2)]
    for k in range(4):
        sy, sz = k // 2, k % 2
        messages.append(((1, 2 * sy - 1, 2 * sz - 1), len(slot_tile), 1))
        slot_tile += [2 * (1 - sy) + 1 - sz]
    for m, (e, start, count) in enumerate(messages):
        for slot in range(start, start + count):
            for p in range(count):
                if m < 3:
                    a = face_first(m, p)
                elif m < 9:
                    a = edge_first(m - 3, p)
                else:
                    a = corner_first(m - 9)
                keys.append((a, SHELL.index(e), slot_tile[slot]))
    for n in range(28):
        a, b = n % 8, (n % 8 + n // 8 + 1) % 8
        keys.append((min(a, b), 0, max(a, b)))
    keys += [(a, 0, a) for a in range(8)]
    assert len(set(keys)) == ENTRIES
    key = np.array([a * 128 + c * 8 + b for a, c, b in keys], np.int32)
    return messages, slot_tile, np.ascontiguousarray(np.broadcast_to(key[:, None], (ENTRIES, 128)))


MESSAGES, SLOT_TILE, KEYS = tables()
N_MSG = len(MESSAGES)


def halves(tile):
    hi = tile.astype(jnp.bfloat16).astype(jnp.float32)
    return hi, (tile - hi)


def two_parts(tile):
    hi, rest = halves(tile)
    return jnp.concatenate([hi, rest], axis=0).astype(jnp.bfloat16)


def three_parts(tile):
    hi, rest = halves(tile)
    mid, low = halves(rest)
    return jnp.concatenate([hi, mid, low, jnp.zeros_like(low)], axis=0)


def fold_parts(parts):
    both = parts[0:8] + parts[8:16]
    if both.shape[1] == 256:
        both = both[:, :128] + both[:, 128:]
    return both


def kernel(sizes, pos, pol, fld, grp, prs, keys, dip_out, res_out,
           hxyz, c3p, xi, mi, ms, f1, g1, f2own, g2own, flag, xj,
           own, vec, polar8, send, halo, back, fold, ar_send, ar_recv,
           hs_sem, hr_sem, fs_sem, fr_sem, as_sem, ar_sem):
    f32, bf16 = jnp.float32, jnp.bfloat16
    nx, ny, nz = sizes
    me = tuple(lax.axis_index(a) for a in AXES)
    gx, gy, gz = me

    def at(e):
        return tuple(lax.rem(m + d + n, n) for m, d, n in zip(me, e, sizes))

    core, zed = lax.rem(gy, 2), gy // 2

    def partner(phase, k):
        if phase == 0:
            j = lax.rem(core * 4 + gz + k, 8)
            return (gx, gy - core + j // 4, lax.rem(j, 4))
        if phase == 1:
            return (lax.rem(gx + k, 8), gy, gz)
        return (gx, lax.rem(zed + k, 8) * 2 + core, gz)

    barrier = pltpu.get_barrier_semaphore()
    signals = 0
    for e, _, _ in MESSAGES:
        for sign in (1, -1):
            pl.semaphore_signal(barrier, inc=1, device_id=at(tuple(sign * d for d in e)), device_id_type=MESH)
            signals += 1
    for phase in range(3):
        for k in range(1, 8):
            pl.semaphore_signal(barrier, inc=1, device_id=partner(phase, k), device_id_type=MESH)
            signals += 1

    row = lax.broadcasted_iota(jnp.int32, (8, 128), 0)
    vec_rows = jnp.logical_and(row >= 4, row < 7)

    def put(x, y, z):
        return jnp.where(row == 4, x, jnp.where(row == 5, y, jnp.where(row == 6, z, 0.0)))

    for a in range(TILES):
        cols = slice(a * TILE, (a + 1) * TILE)
        p = pol[:, cols]
        polar8[a] = jnp.broadcast_to(p, (8, 128))
        own[0, a] = jnp.concatenate(
            [pos[:, cols], lax.rsqrt(p), p * fld[:, cols], grp[:, cols].astype(f32)], axis=0
        )

    def halo_copy(r, m):
        e, start, count = MESSAGES[m]
        return pltpu.make_async_remote_copy(
            src_ref=send.at[r, pl.ds(start, count)], dst_ref=halo.at[r, pl.ds(start, count)],
            send_sem=hs_sem.at[r, m], recv_sem=hr_sem.at[r, m],
            device_id=at(tuple(-d for d in e)), device_id_type=MESH)

    def fold_copy(r, m):
        e, start, count = MESSAGES[m]
        return pltpu.make_async_remote_copy(
            src_ref=back.at[r, pl.ds(start, count)], dst_ref=fold.at[r, pl.ds(start, count)],
            send_sem=fs_sem.at[r, m], recv_sem=fr_sem.at[r, m],
            device_id=at(e), device_id_type=MESH)

    def send_halo(r):
        for slot in range(N_SLOTS):
            send[r, slot] = own[r, SLOT_TILE[slot]]
        for m in range(N_MSG):
            halo_copy(r, m).start()

    for slot in range(N_SLOTS):
        send[0, slot] = own[0, SLOT_TILE[slot]]
    pl.semaphore_wait(barrier, signals)
    for m in range(N_MSG):
        halo_copy(0, m).start()

    key_row = prs[0:1] * 128 + prs[1:2] * 8 + prs[2:3]
    hit = jnp.where(keys[:, : key_row.shape[1]] == key_row, 0.0, FAR)
    flag[...] = jnp.broadcast_to(jnp.min(hit, axis=1, keepdims=True), (ENTRIES, 128))

    def spread(width, first):
        k = lax.broadcasted_iota(jnp.int32, (32, width * 128), 0)
        c = lax.broadcasted_iota(jnp.int32, (32, width * 128), 1) // 128
        return jnp.where(jnp.logical_and(k % 8 == c + first, k < 24), 1.0, 0.0).astype(bf16)

    spread_all = spread(8, 0)
    spread_vec = spread(3, 4)

    def broadcast_own(a, carry):
        cols = jnp.transpose(three_parts(own[0, a])).astype(bf16)
        wide = jnp.dot(cols, spread_all, preferred_element_type=f32)
        xi[a, :, 0:384] = wide[:, 0:384]
        xi[a, :, 384:512] = wide[:, 384:512] * -THOLE_A
        xi[a, :, 512:640] = wide[:, 896:1024]
        mi[a] = wide[:, 512:896]
        parts = two_parts(own[0, a])
        ms[a] = jnp.concatenate([parts, parts], axis=1)
        return carry

    def broadcast_vec(r):
        def one(a, carry):
            cols = jnp.transpose(three_parts(own[r, a])).astype(bf16)
            mi[a] = jnp.dot(cols, spread_vec, preferred_element_type=f32)
            parts = two_parts(own[r, a])
            ms[a] = jnp.concatenate([parts, parts], axis=1)
            return carry

        lax.fori_loop(0, TILES, one, 0)

    lax.fori_loop(0, TILES, broadcast_own, 0)

    def coefficients(n, a, tile, grouped):
        shift = flag[pl.ds(n, 1), :]
        xs = [jnp.broadcast_to(tile[c : c + 1], (16, 128)) for c in range(4)]
        xs[0] = xs[0] + jnp.broadcast_to(shift, (16, 128))
        group = jnp.broadcast_to(tile[7:8], (16, 128))
        for g in range(8):
            rows = slice(16 * g, 16 * g + 16)
            s = [xs[c] - xi[a, rows, c * 128 : c * 128 + 128] for c in range(3)]
            r2 = s[0] * s[0] + s[1] * s[1] + s[2] * s[2]
            if grouped:
                r2 = jnp.where(xi[a, rows, 512:640] == group, FAR * FAR, r2)
            rinv = lax.rsqrt(r2)
            r = r2 * rinv
            x = r2 * r * (xi[a, rows, 384:512] * xs[3])
            ex = jnp.exp(x)
            l3 = 1.0 - ex
            l5 = l3 + x * ex
            v = jnp.clip(r - 8.0, -1.0, 1.0)
            v2 = v * v
            cut = jnp.maximum(0.5 - v * ((v2 * 0.1875 - 0.625) * v2 + 0.9375), 0.0)
            rinv2 = rinv * rinv
            w = cut * (rinv2 * rinv)
            c3 = w * l3
            c5 = (w * 3.0) * rinv2 * l5
            q = c5 * lax.rsqrt(jnp.maximum(c5, 1e-36))
            for c in range(3):
                hxyz[n, c, rows, :] = q * s[c]
            hi = c3.astype(bf16)
            c3p[n, rows, :] = hi
            c3p[n, 128 + 16 * g : 144 + 16 * g, :] = (c3 - hi.astype(f32)).astype(bf16)

    def apply(entries, tile, both=True, first=False):
        mj = [jnp.broadcast_to(tile[4 + c : 5 + c], (8, 128)) for c in range(3)]
        mj_parts = two_parts(tile)
        on_second, c3_second = None, None
        for n, a in entries:
            one = lax.dot_general(mj_parts, c3p[n], (((1,), (1,)), ((), ())), preferred_element_type=f32)
            g1[a] = one if first else g1[a] + one
            if both:
                two = jnp.dot(ms[a], c3p[n], preferred_element_type=f32)
                c3_second = two if c3_second is None else c3_second + two
        for n, a in entries:
            for g in range(16):
                rows = slice(8 * g, 8 * g + 8)
                h = [hxyz[n, c, rows, :] for c in range(3)]
                dj = h[0] * mj[0] + h[1] * mj[1] + h[2] * mj[2]
                for c in range(3):
                    if first:
                        f1[a, c, rows, :] = h[c] * dj
                    else:
                        f1[a, c, rows, :] += h[c] * dj
                if both:
                    m = [mi[a, rows, c * 128 : c * 128 + 128] for c in range(3)]
                    di = h[0] * m[0] + h[1] * m[1] + h[2] * m[2]
                    if on_second is None:
                        on_second = [h[c] * di for c in range(3)]
                    else:
                        on_second = [on_second[c] + h[c] * di for c in range(3)]
        return on_second, c3_second

    def own_pairs(r, low, high):
        def one(k, carry):
            for u in range(4):
                n = k * 4 + u
                a = n % 8
                b = (a + n // 8 + 1) % 8
                tile = own[r, b]
                if r == 0:
                    coefficients(OWN + n, a, tile, True)
                fields, c3_fields = apply([(OWN + n, a)], tile)
                for c in range(3):
                    f2own[b, c] += fields[c]
                g2own[b] += c3_fields
            return carry

        lax.fori_loop(low, high, one, 0)

    def selves(r):
        def one(k, carry):
            for u in range(2):
                a = k * 2 + u
                tile = own[r, a]
                if r == 0:
                    coefficients(SELF + a, a, tile, True)
                apply([(SELF + a, a)], tile, both=False, first=True)
            return carry

        lax.fori_loop(0, 4, one, 0)

    def halo_tiles(r, low, high, entries_of):
        def one(slot, carry):
            entries = entries_of(slot)
            tile = halo[r, slot]
            if r == 0:
                for n, a in entries:
                    coefficients(n, a, xj[slot], False)
            fields, c3_fields = apply(entries, tile)
            back[r, slot] = put(*[jnp.sum(f, axis=0, keepdims=True) for f in fields]) - jnp.where(
                vec_rows, fold_parts(c3_fields), 0.0)
            return carry

        lax.fori_loop(low, high, one, 0)

    def face_entries(slot):
        return [(FACE + slot * 4 + p, face_first(slot // 4, p)) for p in range(4)]

    def edge_entries(slot):
        k = slot - 12
        return [(EDGE + k * 2 + p, edge_first(k // 2, p)) for p in range(2)]

    def corner_entries(slot):
        return [(CORNER + slot - 24, corner_first(slot - 24))]

    ones = jnp.ones((8, 128), f32)

    def run_round(r):
        selves(r)
        own_pairs(r, 0, 4)
        for m in range(N_MSG):
            halo_copy(r, m).wait_recv()
        if r == 0:
            for e, start, count in MESSAGES:
                shift = jnp.where(row == 0, e[0] * BOX_EDGE, 0.0) + jnp.where(
                    row == 1, e[1] * BOX_EDGE, 0.0) + jnp.where(row == 2, e[2] * BOX_EDGE, 0.0)
                for slot in range(start, start + count):
                    xj[slot] = halo[0, slot] + shift
        halo_tiles(r, 0, 12, face_entries)
        for m in range(3):
            fold_copy(r, m).start()
        halo_tiles(r, 12, 24, edge_entries)
        for m in range(3, 9):
            fold_copy(r, m).start()
        halo_tiles(r, 24, 28, corner_entries)
        for m in range(9, 13):
            fold_copy(r, m).start()
        own_pairs(r, 4, 7)

        def gather_own(a, carry):
            lanes = lax.dot_general(
                ones, f1[a].reshape(384, 128), (((1,), (1,)), ((), ())),
                precision=lax.Precision.HIGHEST, preferred_element_type=f32)
            total = put(*[
                lanes[:, c * 128 : c * 128 + 128] + jnp.sum(f2own[a, c], axis=0, keepdims=True)
                for c in range(3)])
            vec[r, a] = total - jnp.where(vec_rows, fold_parts(g1[a]) + fold_parts(g2own[a]), 0.0)
            return carry

        lax.fori_loop(0, TILES, gather_own, 0)

    def add_folded(r):
        for m in range(N_MSG):
            fold_copy(r, m).wait_recv()
        for slot in range(N_SLOTS):
            vec[r, SLOT_TILE[slot]] += fold[r, slot]

    def clear():
        f2own[...] = jnp.zeros_like(f2own)
        g2own[...] = jnp.zeros_like(g2own)

    def rows_dot(left, right):
        total = left(0) * right(0)
        for a in range(1, TILES):
            total = total + left(a) * right(a)
        return total

    for r in range(3):
        if r > 0:
            broadcast_vec(r)
        clear()
        run_round(r)
        if r < 2:
            add_folded(r)
            for a in range(TILES):
                own[r + 1, a] = polar8[a] * vec[r, a]
            send_halo(r + 1)

    g00 = rows_dot(lambda a: vec[0, a], lambda a: own[1, a])
    g01 = rows_dot(lambda a: vec[1, a], lambda a: own[1, a])
    g11 = rows_dot(lambda a: vec[1, a], lambda a: own[2, a])
    g12 = rows_dot(lambda a: vec[2, a], lambda a: own[2, a])
    for slot in range(N_SLOTS):
        g12 = g12 + halo[2, slot] * back[2, slot]

    def phase_copy(phase, k):
        return pltpu.make_async_remote_copy(
            src_ref=ar_send.at[phase], dst_ref=ar_recv.at[phase, k - 1],
            send_sem=as_sem.at[phase, k - 1], recv_sem=ar_sem.at[phase, k - 1],
            device_id=partner(phase, k), device_id_type=MESH)

    parts = [jnp.sum(g, axis=0, keepdims=True) for g in (g00, g01, g11, g12)]
    total = jnp.where(row == 0, parts[0], jnp.where(row == 1, parts[1], jnp.where(row == 2, parts[2], parts[3])))
    for phase in range(3):
        ar_send[phase] = total
        for k in range(1, 8):
            phase_copy(phase, k).start()
        if phase == 0:
            add_folded(2)
        for k in range(1, 8):
            phase_copy(phase, k).wait_recv()
            total = total + ar_recv[phase, k - 1]

    sums = jnp.sum(total, axis=1, keepdims=True)
    s00, s01, s11, s12 = (sums[i : i + 1] for i in range(4))
    alpha = s00 / (s00 - s01)
    keep = 1.0 - alpha
    rho = keep * keep * s00 + 2.0 * keep * alpha * s01 + alpha * alpha * s11
    a0 = keep + rho / s00
    a1 = alpha
    denom = (a0 * a0 * s00 + 2.0 * a0 * a1 * s01 + a1 * a1 * s11) - (
        a0 * a0 * s01 + 2.0 * a0 * a1 * s11 + a1 * a1 * s12)
    step = rho / denom
    d1, d2 = alpha + step * a0, step * a1
    r0, r1, r2 = keep - step * a0, alpha - step * a1 + step * a0, step * a1
    for a in range(TILES):
        cols = slice(a * TILE, (a + 1) * TILE)
        dip = own[0, a] + d1 * own[1, a] + d2 * own[2, a]
        res = r0 * vec[0, a] + r1 * vec[1, a] + r2 * vec[2, a]
        dip_out[:, cols] = dip[4:7]
        res_out[:, cols] = res[4:7]

    for r in range(3):
        for m in range(N_MSG):
            halo_copy(r, m).wait_send()
            fold_copy(r, m).wait_send()
    for phase in range(3):
        for k in range(1, 8):
            phase_copy(phase, k).wait_send()


def solution(mesh):
    sizes = tuple(mesh.shape[a] for a in AXES)
    f32, bf16 = jnp.float32, jnp.bfloat16

    def shards(positions, polar, field, groups, pair_tiles):
        vmem = pl.BlockSpec(memory_space=pltpu.VMEM)
        dma = pltpu.SemaphoreType.DMA
        scratch = [
            pltpu.VMEM((ENTRIES, 3, 128, 128), f32),
            pltpu.VMEM((ENTRIES, 256, 128), bf16),
            pltpu.VMEM((8, 128, 640), f32),
            pltpu.VMEM((8, 128, 384), f32),
            pltpu.VMEM((8, 16, 256), bf16),
            pltpu.VMEM((8, 3, 128, 128), f32),
            pltpu.VMEM((8, 16, 256), f32),
            pltpu.VMEM((8, 3, 8, 128), f32),
            pltpu.VMEM((8, 16, 128), f32),
            pltpu.VMEM((ENTRIES, 128), f32),
            pltpu.VMEM((N_SLOTS, 8, 128), f32),
            pltpu.VMEM((3, 8, 8, 128), f32),
            pltpu.VMEM((3, 8, 8, 128), f32),
            pltpu.VMEM((8, 8, 128), f32),
            pltpu.VMEM((3, N_SLOTS, 8, 128), f32),
            pltpu.VMEM((3, N_SLOTS, 8, 128), f32),
            pltpu.VMEM((3, N_SLOTS, 8, 128), f32),
            pltpu.VMEM((3, N_SLOTS, 8, 128), f32),
            pltpu.VMEM((3, 8, 128), f32),
            pltpu.VMEM((3, 7, 8, 128), f32),
            dma((3, N_MSG)), dma((3, N_MSG)), dma((3, N_MSG)), dma((3, N_MSG)),
            dma((3, 7)), dma((3, 7)),
        ]
        atoms = positions.shape[-1]
        out = jax.ShapeDtypeStruct((3, atoms), f32)
        dip, res = pl.pallas_call(
            functools.partial(kernel, sizes),
            out_shape=(out, out),
            in_specs=[vmem] * 6,
            out_specs=(vmem, vmem),
            scratch_shapes=scratch,
            compiler_params=pltpu.CompilerParams(
                collective_id=0, has_side_effects=True, vmem_limit_bytes=50 * 1024 * 1024),
            name="dipole_cg",
        )(positions.reshape(3, atoms), polar.reshape(1, atoms), field.reshape(3, atoms),
          groups.reshape(1, atoms), pair_tiles.reshape(3, -1), jnp.asarray(KEYS))
        return dip.reshape(1, 1, 1, 3, atoms), res.reshape(1, 1, 1, 3, atoms)

    placed = (
        P(*AXES, None, None), P(*AXES, None), P(*AXES, None, None), P(*AXES, None), P(*AXES, None, None))
    return jax.shard_map(
        shards, mesh=mesh, in_specs=placed, out_specs=(placed[0], placed[0]), check_vma=False)
```

time: 915 us -> 88.4 us (0.10)
  blocking collectives: 292 us -> 0 us
  other arithmetic: 202 us -> 0 us
  starting transfers between devices: 192 us -> 0 us
  local copies, waits for them, and re-layouts: 177 us -> 2.7 us
  Pallas kernels: 0 us -> 84.8 us
  waiting for transfers between devices: 39 us -> 0 us
    psum x3 -> x0, blocking collectives: 292 us -> none  [the longest x2 194 us: residual_sum(): return lax.psum(jnp.sum(residual * precond), ('gx', 'gy', 'gz'))]
    ppermute x35 -> x0, starting transfers between devices: 192 us -> none  [the longest x19 146 us: from_behind(): lax.ppermute(array, axis, [(i, (i + by) % length) for i in range(length)])]
    gather x363 -> x0, local copies, waits for them, and re-layouts: 172 us -> none  [the longest x33 21.2 us: one_block(): grid_slot = slot_of_code[jnp.minimum(near_code, 13)]]
    reduce_sum x70 -> x0, other arithmetic: 89.5 us -> none  [the longest x33 50.9 us: field_second(): jnp.sum(coef_five * along * separation - coef_three * first_dip[:, :, :,...]
    pallas_call x0 -> x1, Pallas kernels: none -> 84.8 us  [shards(): pl.pallas_call(functools.partial(kernel, sizes), out_shape=(out, out), in...]
    scatter-add x66 -> x0, other arithmetic: 54 us -> none  [the longest x33 28 us: one_block(): far_field.at[grid_slot, :, second_tile]]
    mul x102 -> x0, other arithmetic: 51.5 us -> none  [the longest x33 47.6 us: field_first(): coef_five * along * separation - coef_three * second_dip[:, :, None, :]]
    ppermute x35 -> x0, waiting for transfers between devices: 39 us -> none  [the longest x19 32.7 us: from_behind(): lax.ppermute(array, axis, [(i, (i + by) % length) for i in range(length)])]
  transfers between devices with their start and end apart: 35 -> 0, of which waited for: 21 -> 0; matrix products, arithmetic and copies ran while one was open for 0% -> 0% of each run, Pallas kernels for 0% -> 0%
where the time goes in v1:
time: 88.4 us; the launch traced here: 88.2 us
  Pallas kernels  84.8 us (96%)
  local copies, waits for them, and re-layouts  2.7 us (3%)
    pallas_call x1, Pallas kernels, shards(): pl.pallas_call(functools.partial(kernel, sizes), out_shape=(out, out), in...  84.8 us
    unnamed x10, local copies, waits for them, and re-layouts  2.7 us

profile of v1, /device:TPU:1, one launch (start us, length us, event | category | flops | bytes accessed | tf_op | source)
XLA Modules:
  0.0 88.2 jit_solution(12045439320590358179)
XLA Ops:
  0.6 0.0 copy-start
  0.6 0.7 copy.16
  1.3 0.0 copy-start.1
  1.3 0.0 copy-start.2
  1.3 0.8 copy_bitcast_fusion
  2.1 0.0 copy-done
  2.1 0.0 copy-done.1
  2.1 0.0 copy-done.2
  2.1 84.8 %dipole_cg.1 = (f32[3,1024]{1,0:T(4,128)S(1)}, f32[3,1024]{1,0:T(4,128)S(1)}) custom-call(f32[3,1024]{1,0:T(4,128)S(1)} %get-tuple-element.9.pos, f32[1,1024]{1,0:T(1,128)S(1)} %bitcast.14, f32[3,1024]{1,0:T(4,128)S(1)} %get-tuple-element.8.fld, s32[1,1024]{1,0:T(1,128)S(1)} %bitcast.15, s32[3,112]{1,0:T(4,128)S(1)} %bitcast.13, s32[112,128]{1,0:T(8,128)S(1)} %copy-done), custom_call_target="tpu_custom_call" | custom-call | tf_op jit(solution)/shard_map/dipole_cg/pallas_call | solution.py:476
  87.0 0.6 copy.8
  87.6 0.6 copy.9
Async XLA Ops:
  0.6 1.5 %copy-start = (s32[112,128]{1,0:T(8,128)S(1)}, s32[112,128]{1,0:T(8,128)}, u32[]{:S(2)}) copy-start(s32[112,128]{1,0:T(8,128)} %constant.2.clone.keys) | copy-start | bytes 172036
  1.3 0.8 copy-start.1
  1.3 0.8 copy-start.2

commit v2 on v1

v2 whole, which is shorter than its diff:
```python
import functools

import jax
import jax.numpy as jnp
import numpy as np
from jax import lax
from jax.experimental import pallas as pl
from jax.experimental.pallas import tpu as pltpu
from jax.sharding import PartitionSpec as P

TILE = 128
TILES = 8
AXES = ("gx", "gy", "gz")
BOX_EDGE = 21.7
THOLE_A = 0.39
FAR = 1000.0
SCALE = 3.0 / 16.0
C10 = np.float32(10.0 / 3.0)
C8 = np.float32(5.0) - (C10 - np.float32(1.0))
MESH = pl.DeviceIdType.MESH
SHELL = [
    (0, 0, 0), (0, 0, 1), (0, 1, -1), (0, 1, 0), (0, 1, 1), (1, -1, -1), (1, -1, 0),
    (1, -1, 1), (1, 0, -1), (1, 0, 0), (1, 0, 1), (1, 1, -1), (1, 1, 0), (1, 1, 1),
]
N_SLOTS = 28
FACE, EDGE, CORNER, OWN, LAST = 0, 48, 72, 76, 108
ENTRIES = 112


def face_first(f, p):
    s = 1 + f + f * (f - 1) // 2
    return p // s * (2 * s) + s + p % s


def edge_first(k, p):
    g, sg = k // 2, k % 2
    free = 4 - 2 * g + g * (g - 1) // 2
    return free * p + 4 - 2 * ((2 - g) // 2) + (1 + g // 2) * sg


def corner_first(k):
    return 4 + k


def tables():
    messages, slot_tile, keys = [], [], []
    for f in range(3):
        s = 1 << f
        e = [0, 0, 0]
        e[2 - f] = 1
        messages.append((tuple(e), len(slot_tile), 4))
        slot_tile += [q // s * 2 * s + q % s for q in range(4)]
    for k in range(6):
        g, sg = k // 2, k % 2
        e = [[0, 1, 2 * sg - 1], [1, 0, 2 * sg - 1], [1, 2 * sg - 1, 0]][g]
        free, low = (4, 2, 1)[g], (1, 1, 2)[g]
        messages.append((tuple(e), len(slot_tile), 2))
        slot_tile += [free * q + low * (1 - sg) for q in range(2)]
    for k in range(4):
        sy, sz = k // 2, k % 2
        messages.append(((1, 2 * sy - 1, 2 * sz - 1), len(slot_tile), 1))
        slot_tile += [2 * (1 - sy) + 1 - sz]
    for m, (e, start, count) in enumerate(messages):
        for p in range(count):
            if m < 3:
                a = face_first(m, p)
            elif m < 9:
                a = edge_first(m - 3, p)
            else:
                a = corner_first(m - 9)
            keys += [(a, SHELL.index(e), slot_tile[start + q]) for q in range(count)]
    for a in range(8):
        for d in range(4):
            b = (a + d) % 8
            keys.append((min(a, b), 0, max(a, b)))
    keys += [(a, 0, a + 4) for a in range(4)]
    assert len(set(keys)) == ENTRIES
    key = np.array([a * 128 + c * 8 + b for a, c, b in keys], np.int32)
    return messages, slot_tile, np.ascontiguousarray(np.broadcast_to(key[:, None], (ENTRIES, 128)))


MESSAGES, SLOT_TILE, KEYS = tables()
N_MSG = len(MESSAGES)


def halves(tile):
    hi = tile.astype(jnp.bfloat16).astype(jnp.float32)
    return hi, (tile - hi)


def two_parts(tile):
    hi, rest = halves(tile)
    return jnp.concatenate([hi, rest], axis=0).astype(jnp.bfloat16)


def fold_parts(parts):
    return parts[0:8] + parts[8:16]


def kernel(sizes, pos, pol, fld, grp, prs, keys, dip_out, res_out,
           hxyz, c3p, xi, mi, ms, mjp, f1, g1, f2own, g2own, flag, xj,
           own, vec, polar8, send, halo, back, fold, ar_send, ar_recv,
           hs_sem, hr_sem, fs_sem, fr_sem, as_sem, ar_sem):
    f32, bf16 = jnp.float32, jnp.bfloat16
    me = tuple(lax.axis_index(a) for a in AXES)
    gx, gy, gz = me

    def at(e):
        return tuple(lax.rem(m + d + n, n) for m, d, n in zip(me, e, sizes))

    core, zed = lax.rem(gy, 2), gy // 2

    def partner(phase, k):
        if phase == 0:
            j = lax.rem(core * 4 + gz + k, 8)
            return (gx, gy - core + j // 4, lax.rem(j, 4))
        if phase == 1:
            return (lax.rem(gx + k, 8), gy, gz)
        return (gx, lax.rem(zed + k, 8) * 2 + core, gz)

    barrier = pltpu.get_barrier_semaphore()
    signals = 0
    for e, _, _ in MESSAGES:
        for sign in (1, -1):
            pl.semaphore_signal(barrier, inc=1, device_id=at(tuple(sign * d for d in e)), device_id_type=MESH)
            signals += 1
    for phase in range(3):
        for k in range(1, 8):
            pl.semaphore_signal(barrier, inc=1, device_id=partner(phase, k), device_id_type=MESH)
            signals += 1

    row = lax.broadcasted_iota(jnp.int32, (8, 128), 0)
    vec_rows = jnp.logical_and(row >= 4, row < 7)

    def put(x, y, z):
        return jnp.where(row == 4, x, jnp.where(row == 5, y, jnp.where(row == 6, z, 0.0)))

    def tile_field(sums, parts):
        rows = [jnp.sum(f, axis=0, keepdims=True) for f in sums]
        return put(*rows) - jnp.where(vec_rows, fold_parts(parts), 0.0)

    for a in range(TILES):
        p = pol[a : a + 1]
        polar8[a] = jnp.broadcast_to(p * SCALE, (8, 128))
        own[0, a] = jnp.concatenate(
            [pos[8 * c + a : 8 * c + a + 1] for c in range(3)] + [lax.rsqrt(p)]
            + [p * SCALE * fld[8 * c + a : 8 * c + a + 1] for c in range(3)]
            + [grp[a : a + 1].astype(f32)], axis=0)

    def halo_copy(r, m):
        e, start, count = MESSAGES[m]
        return pltpu.make_async_remote_copy(
            src_ref=send.at[r, pl.ds(start, count)], dst_ref=halo.at[r, pl.ds(start, count)],
            send_sem=hs_sem.at[r, m], recv_sem=hr_sem.at[r, m],
            device_id=at(tuple(-d for d in e)), device_id_type=MESH)

    def fold_copy(r, m):
        e, start, count = MESSAGES[m]
        return pltpu.make_async_remote_copy(
            src_ref=back.at[r, pl.ds(start, count)], dst_ref=fold.at[r, pl.ds(start, count)],
            send_sem=fs_sem.at[r, m], recv_sem=fr_sem.at[r, m],
            device_id=at(e), device_id_type=MESH)

    def send_halo(r):
        for slot in range(N_SLOTS):
            send[r, slot] = own[r, SLOT_TILE[slot]]
        if r == 0:
            pl.semaphore_wait(barrier, signals)
        for m in range(N_MSG):
            halo_copy(r, m).start()

    send_halo(0)

    key_row = prs[0] * 128 + prs[1] * 8 + prs[2]
    hit = jnp.where(keys[:, : key_row.shape[1]] == key_row, 0.0, FAR)
    flag[...] = jnp.broadcast_to(jnp.min(hit, axis=1, keepdims=True), (ENTRIES, 128))

    def columns(r):
        cols = jnp.transpose(own[r].reshape(64, 128))
        for a in range(TILES):
            def wide(k, scale):
                return jnp.broadcast_to(cols[:, a * 8 + k : a * 8 + k + 1] * scale, (128, 128))

            for c in range(3):
                mi[a, :, c * 128 : c * 128 + 128] = wide(4 + c, 3.0)
            if r == 0:
                for c in range(3):
                    xi[a, :, c * 128 : c * 128 + 128] = wide(c, 1.0)
                xi[a, :, 384:512] = wide(3, -THOLE_A)
                xi[a, :, 512:640] = wide(7, 1.0)
            parts = two_parts(own[r, a])
            ms[a] = jnp.concatenate([parts, parts], axis=1)

    def coefficients(n, a, tile, grouped):
        shift = flag[pl.ds(n, 1), :]
        xs = [jnp.broadcast_to(tile[c : c + 1], (16, 128)) for c in range(4)]
        xs[0] = xs[0] + jnp.broadcast_to(shift, (16, 128))
        group = jnp.broadcast_to(tile[7:8], (16, 128))
        for g in range(8):
            rows = slice(16 * g, 16 * g + 16)
            s = [xs[c] - xi[a, rows, c * 128 : c * 128 + 128] for c in range(3)]
            r2 = s[0] * s[0] + s[1] * s[1] + s[2] * s[2]
            if grouped:
                r2 = jnp.where(xi[a, rows, 512:640] == group, FAR * FAR, r2)
            rinv = lax.rsqrt(r2)
            r = r2 * rinv
            x = r2 * r * (xi[a, rows, 384:512] * xs[3])
            ex = jnp.exp(x)
            l3 = 1.0 - ex
            v = jnp.clip(r - 8.0, -1.0, 1.0)
            v2 = v * v
            cut = jnp.maximum(C8 - v * ((v2 - C10) * v2 + 5.0), 0.0)
            w = cut * (rinv * rinv * rinv)
            c3 = w * l3
            q2 = w * (l3 + x * ex)
            q = q2 * lax.rsqrt(jnp.maximum(q2, 1e-36)) * rinv
            for c in range(3):
                hxyz[n, c, rows, :] = q * s[c]
            hi = c3.astype(bf16)
            c3p[n, rows, :] = hi
            c3p[n, 128 + 16 * g : 144 + 16 * g, :] = (c3 - hi.astype(f32)).astype(bf16)

    def beside(ns):
        return jnp.concatenate([c3p[n] for n in ns], axis=1) if len(ns) > 1 else c3p[ns[0]]

    def dot_rows(h, m):
        return h[0] * m[0] + h[1] * m[1] + h[2] * m[2]

    def on_seconds(firsts):
        count = len(firsts[0][1])
        sums, parts = [None] * count, None
        for a, ns in firsts:
            part = jnp.dot(ms[a], beside(ns), preferred_element_type=f32)
            parts = part if parts is None else parts + part
        for a, ns in firsts:
            for g in range(16):
                rows = slice(8 * g, 8 * g + 8)
                m = [mi[a, rows, c * 128 : c * 128 + 128] for c in range(3)]
                for q in range(count):
                    h = [hxyz[ns[q], c, rows, :] for c in range(3)]
                    d = dot_rows(h, m)
                    add = [h[c] * d for c in range(3)]
                    sums[q] = add if sums[q] is None else [sums[q][c] + add[c] for c in range(3)]
        return [(sums[q], parts[:, q * 128 : q * 128 + 128]) for q in range(count)]

    def triple(tile):
        return [jnp.broadcast_to(tile[4 + c : 5 + c] * 3.0, (8, 128)) for c in range(3)]

    def on_firsts(firsts, tiles, rows_of_parts):
        mj = [triple(t) for t in tiles]
        for a, ns in firsts:
            g1[a] += lax.dot_general(
                rows_of_parts, beside(ns), (((1,), (1,)), ((), ())), preferred_element_type=f32)
        for a, ns in firsts:
            for g in range(16):
                rows = slice(8 * g, 8 * g + 8)
                sums = [f1[a, c, rows, :] for c in range(3)]
                for q, n in enumerate(ns):
                    h = [hxyz[n, c, rows, :] for c in range(3)]
                    d = dot_rows(h, mj[q])
                    sums = [sums[c] + h[c] * d for c in range(3)]
                for c in range(3):
                    f1[a, c, rows, :] = sums[c]

    def face_list(f):
        return [(face_first(f, p), [FACE + (f * 4 + p) * 4 + q for q in range(4)]) for p in range(4)]

    def edge_list(k):
        return [(edge_first(k, p), [EDGE + (k * 2 + p) * 2 + q for q in range(2)]) for p in range(2)]

    def corner_list(k):
        return [(corner_first(k), [CORNER + k])]

    kinds = ((0, 3, 4, 0, face_list, 1), (3, 9, 2, 12, edge_list, 2), (9, 13, 1, 24, corner_list, 4))

    def send_back(r):
        for low, high, count, start, entries, group in kinds:
            def one(step, carry):
                for k in [step * group + u for u in range(group)]:
                    fields = on_seconds(entries(k))
                    for q in range(count):
                        back[r, start + k * count + q] = tile_field(*fields[q])
                return carry

            lax.fori_loop(0, (high - low) // group, one, 0)
            for m in range(low, high):
                fold_copy(r, m).start()

    def take_halo(r, kind):
        low, high, count, start, entries, group = kinds[kind]

        def one(step, carry):
            for k in [step * group + u for u in range(group)]:
                slots = [start + k * count + q for q in range(count)]
                parts = [mjp[s] for s in slots]
                wide = jnp.concatenate(parts, axis=1) if count > 1 else parts[0]
                on_firsts(entries(k), [halo[r, s] for s in slots], wide)
            return carry

        lax.fori_loop(0, (high - low) // group, one, 0)

    def own_tiles(r):
        f2own[...] = jnp.zeros_like(f2own)
        g2own[...] = jnp.zeros_like(g2own)

        def near(a, carry):
            ns = [OWN + a * 4 + d for d in range(4)]
            bs = [lax.rem(a + d, 8) for d in range(4)]
            tiles = [own[r, b] for b in bs]
            mj = [triple(t) for t in tiles]
            two = jnp.dot(ms[a], beside(ns), preferred_element_type=f32)
            wide = jnp.concatenate([ms[b, :, 0:128] for b in bs[1:]], axis=1)
            g1[a] = lax.dot_general(
                wide, beside(ns[1:]), (((1,), (1,)), ((), ())), preferred_element_type=f32)
            sums = [[jnp.zeros((8, 128), f32)] * 3 for _ in range(4)]
            for g in range(16):
                rows = slice(8 * g, 8 * g + 8)
                m = [mi[a, rows, c * 128 : c * 128 + 128] for c in range(3)]
                first = None
                for d in range(4):
                    h = [hxyz[ns[d], c, rows, :] for c in range(3)]
                    t = dot_rows(h, m)
                    sums[d] = [sums[d][c] + h[c] * t for c in range(3)]
                    if d > 0:
                        t = dot_rows(h, mj[d])
                        add = [h[c] * t for c in range(3)]
                        first = add if first is None else [first[c] + add[c] for c in range(3)]
                for c in range(3):
                    f1[a, c, rows, :] = first[c]
            vec[r, a] = tile_field(sums[0], two[:, 0:128])
            for d in range(1, 4):
                for c in range(3):
                    f2own[bs[d], c] += sums[d][c]
                g2own[bs[d]] += two[:, d * 128 : d * 128 + 128]
            return carry

        lax.fori_loop(0, TILES, near, 0)

        for a in range(4):
            entry = [(a, [LAST + a])]
            fields, parts = on_seconds(entry)[0]
            for c in range(3):
                f2own[a + 4, c] += fields[c]
            g2own[a + 4] += parts
            on_firsts(entry, [own[r, a + 4]], ms[a + 4, :, 0:128])

    def own_sums(r):
        total = jnp.zeros((8, 128), f32)
        for a in range(TILES):
            off = tile_field([f2own[a, c] for c in range(3)], g2own[a])
            total = total + own[r, a] * (vec[r, a] + 2.0 * off)
            vec[r, a] += off
        return total

    def wait_halo(r):
        for m in range(N_MSG):
            halo_copy(r, m).wait_recv()
        for slot in range(N_SLOTS):
            mjp[slot] = two_parts(halo[r, slot])

    def first_sums(r):
        for a in range(TILES):
            sums = [jnp.sum(jnp.transpose(f1[a, c]), axis=0, keepdims=True) for c in range(3)]
            parts = fold_parts(g1[a])
            vec[r, a] += put(*sums) - jnp.where(vec_rows, parts[:, :128] + parts[:, 128:], 0.0)

    def add_folded(r):
        for m in range(N_MSG):
            fold_copy(r, m).wait_recv()
        for slot in range(N_SLOTS):
            vec[r, SLOT_TILE[slot]] += fold[r, slot]

    def phase_copy(phase, k):
        return pltpu.make_async_remote_copy(
            src_ref=ar_send.at[phase], dst_ref=ar_recv.at[phase, k - 1],
            send_sem=as_sem.at[phase, k - 1], recv_sem=ar_sem.at[phase, k - 1],
            device_id=partner(phase, k), device_id_type=MESH)

    def start_phase(phase, total):
        ar_send[phase] = total
        for k in range(1, 8):
            phase_copy(phase, k).start()

    def end_phase(phase):
        total = ar_send[phase]
        for k in range(1, 8):
            phase_copy(phase, k).wait_recv()
            total = total + ar_recv[phase, k - 1]
        return total

    def rows_dot(left, right):
        total = left[0] * right[0]
        for a in range(1, TILES):
            total = total + left[a] * right[a]
        return total

    columns(0)

    def own_near(a, carry):
        for d in range(4):
            coefficients(OWN + a * 4 + d, a, own[0, lax.rem(a + d, 8)], True)
        return carry

    lax.fori_loop(0, 8, own_near, 0)
    for a in range(4):
        coefficients(LAST + a, a, own[0, a + 4], True)
    own_tiles(0)
    own_sums(0)
    wait_halo(0)
    for e, start, count in MESSAGES:
        shift = jnp.where(row == 0, e[0] * BOX_EDGE, 0.0) + jnp.where(
            row == 1, e[1] * BOX_EDGE, 0.0) + jnp.where(row == 2, e[2] * BOX_EDGE, 0.0)
        for slot in range(start, start + count):
            xj[slot] = halo[0, slot] + shift

    def face_one(n, carry):
        f = n // 4
        for q in range(4):
            coefficients(FACE + n * 4 + q, face_first(f, n % 4), xj[f * 4 + q], False)
        return carry

    def edge_one(k, carry):
        for p in range(2):
            for q in range(2):
                coefficients(EDGE + k * 4 + p * 2 + q, edge_first(k, p), xj[12 + k * 2 + q], False)
        return carry

    lax.fori_loop(0, 12, face_one, 0)
    lax.fori_loop(0, 6, edge_one, 0)
    for k in range(4):
        coefficients(CORNER + k, corner_first(k), xj[24 + k], False)
    send_back(0)
    for kind in range(3):
        take_halo(0, kind)
    first_sums(0)
    add_folded(0)

    for r in (1, 2):
        for a in range(TILES):
            own[r, a] = polar8[a] * vec[r - 1, a]
        send_halo(r)
        columns(r)
        send_back(r)
        own_tiles(r)
        g12 = own_sums(r)
        wait_halo(r)
        if r == 2:
            for slot in range(N_SLOTS):
                g12 = g12 + 2.0 * (halo[2, slot] * back[2, slot])
            parts = [
                rows_dot(vec[0], own[1]), rows_dot(vec[1], own[1]), rows_dot(vec[1], own[2]), g12]
            parts = [jnp.sum(g, axis=0, keepdims=True) for g in parts]
            start_phase(0, jnp.where(row == 0, parts[0], jnp.where(
                row == 1, parts[1], jnp.where(row == 2, parts[2], parts[3]))))
        take_halo(r, 0)
        if r == 2:
            start_phase(1, end_phase(0))
        take_halo(r, 1)
        take_halo(r, 2)
        if r == 2:
            start_phase(2, end_phase(1))
        first_sums(r)
        add_folded(r)

    sums = jnp.sum(end_phase(2), axis=1, keepdims=True)
    s00, s01, s11, s12 = (sums[i : i + 1] for i in range(4))
    alpha = s00 / (s00 - s01)
    keep = 1.0 - alpha
    rho = keep * keep * s00 + 2.0 * keep * alpha * s01 + alpha * alpha * s11
    a0 = keep + rho / s00
    a1 = alpha
    denom = (a0 * a0 * s00 + 2.0 * a0 * a1 * s01 + a1 * a1 * s11) - (
        a0 * a0 * s01 + 2.0 * a0 * a1 * s11 + a1 * a1 * s12)
    step = rho / denom
    d0 = 1.0 / SCALE
    d1, d2 = (alpha + step * a0) * d0, step * a1 * d0
    r0, r1, r2 = keep - step * a0, alpha - step * a1 + step * a0, step * a1
    for a in range(TILES):
        dip = d0 * own[0, a] + d1 * own[1, a] + d2 * own[2, a]
        res = r0 * vec[0, a] + r1 * vec[1, a] + r2 * vec[2, a]
        for c in range(3):
            dip_out[8 * c + a : 8 * c + a + 1] = dip[4 + c : 5 + c]
            res_out[8 * c + a : 8 * c + a + 1] = res[4 + c : 5 + c]

    for r in range(3):
        for m in range(N_MSG):
            halo_copy(r, m).wait_send()
            fold_copy(r, m).wait_send()
    for phase in range(3):
        for k in range(1, 8):
            phase_copy(phase, k).wait_send()


def solution(mesh):
    sizes = tuple(mesh.shape[a] for a in AXES)
    f32, bf16 = jnp.float32, jnp.bfloat16

    def shards(positions, polar, field, groups, pair_tiles):
        vmem = pl.BlockSpec(memory_space=pltpu.VMEM)
        dma = pltpu.SemaphoreType.DMA
        scratch = [
            pltpu.VMEM((ENTRIES, 3, 128, 128), f32),
            pltpu.VMEM((ENTRIES, 256, 128), bf16),
            pltpu.VMEM((8, 128, 640), f32),
            pltpu.VMEM((8, 128, 384), f32),
            pltpu.VMEM((8, 16, 256), bf16),
            pltpu.VMEM((N_SLOTS, 16, 128), bf16),
            pltpu.VMEM((8, 3, 128, 128), f32),
            pltpu.VMEM((8, 16, 256), f32),
            pltpu.VMEM((8, 3, 8, 128), f32),
            pltpu.VMEM((8, 16, 128), f32),
            pltpu.VMEM((ENTRIES, 128), f32),
            pltpu.VMEM((N_SLOTS, 8, 128), f32),
            pltpu.VMEM((3, 8, 8, 128), f32),
            pltpu.VMEM((3, 8, 8, 128), f32),
            pltpu.VMEM((8, 8, 128), f32),
            pltpu.VMEM((3, N_SLOTS, 8, 128), f32),
            pltpu.VMEM((3, N_SLOTS, 8, 128), f32),
            pltpu.VMEM((3, N_SLOTS, 8, 128), f32),
            pltpu.VMEM((3, N_SLOTS, 8, 128), f32),
            pltpu.VMEM((3, 8, 128), f32),
            pltpu.VMEM((3, 7, 8, 128), f32),
            dma((3, N_MSG)), dma((3, N_MSG)), dma((3, N_MSG)), dma((3, N_MSG)),
            dma((3, 7)), dma((3, 7)),
        ]
        atoms = positions.shape[-1]
        rows = atoms // TILE
        out = jax.ShapeDtypeStruct((3 * rows, TILE), f32)
        dip, res = pl.pallas_call(
            functools.partial(kernel, sizes),
            out_shape=(out, out),
            in_specs=[vmem] * 6,
            out_specs=(vmem, vmem),
            scratch_shapes=scratch,
            compiler_params=pltpu.CompilerParams(
                collective_id=0, has_side_effects=True, vmem_limit_bytes=50 * 1024 * 1024),
            name="dipole_cg",
        )(positions.reshape(3 * rows, TILE), polar.reshape(rows, TILE), field.reshape(3 * rows, TILE),
          groups.reshape(rows, TILE), pair_tiles.reshape(3, 1, -1), jnp.asarray(KEYS))
        return dip.reshape(1, 1, 1, 3, atoms), res.reshape(1, 1, 1, 3, atoms)

    placed = (
        P(*AXES, None, None), P(*AXES, None), P(*AXES, None, None), P(*AXES, None), P(*AXES, None, None))
    return jax.shard_map(
        shards, mesh=mesh, in_specs=placed, out_specs=(placed[0], placed[0]), check_vma=False)
```

time: 88.4 us -> 71.8 us (0.81)
  Pallas kernels: 84.8 us -> 65.6 us
  local copies, waits for them, and re-layouts: 2.7 us -> 4.8 us
    pallas_call x1, Pallas kernels: 84.8 us -> 65.6 us  [shards(): pl.pallas_call(functools.partial(kernel, sizes), out_shape=(out, out), in...]
    unnamed x10 -> x14, local copies, waits for them, and re-layouts: 2.7 us -> 4.8 us
where the time goes in v2:
time: 71.8 us; the launch traced here: 71.1 us
  Pallas kernels  65.6 us (91%)
  local copies, waits for them, and re-layouts  4.8 us (7%)
    pallas_call x1, Pallas kernels, shards(): pl.pallas_call(functools.partial(kernel, sizes), out_shape=(out, out), in...  65.6 us
    unnamed x14, local copies, waits for them, and re-layouts  4.8 us

profile of v2, /device:TPU:1, one launch (start us, length us, event | category | flops | bytes accessed | tf_op | source)
XLA Modules:
  0.0 71.1 jit_solution(1325335290864264343)
XLA Ops:
  0.6 0.0 copy-start.4
  0.6 0.0 copy-start.3
  0.7 0.7 copy-done.4
  1.3 0.0 copy-done.3
  1.3 0.0 copy-start
  1.3 0.8 %copy-done = s32[112,128]{1,0:T(8,128)S(1)} copy-done((s32[112,128]{1,0:T(8,128)S(1)}, s32[112,128]{1,0:T(8,128)}, u32[]{:S(2)}) %copy-start) | copy-done | bytes 57368
  2.2 0.0 copy-start.1
  2.2 0.7 copy-done.1
  2.9 0.0 copy-start.2
  2.9 0.7 copy-done.2
  3.6 0.0 copy-start.5
  3.6 0.7 copy-done.5
  4.2 65.6 %dipole_cg.1 = (f32[24,128]{1,0:T(8,128)S(1)}, f32[24,128]{1,0:T(8,128)S(1)}) custom-call(f32[24,128]{1,0:T(8,128)S(1)} %bitcast.9, f32[8,128]{1,0:T(8,128)S(1)} %bitcast.11, f32[24,128]{1,0:T(8,128)S(1)} %bitcast.10, s32[8,128]{1,0:T(8,128)S(1)} %bitcast.12, s32[3,1,112]{2,1,0:T(1,128)S(1)} %bitcast.13, s32[112,128]{1,0:T(8,128)S(1)} %copy-done), custom_call_target="tpu_custom_call" | custom-call | tf_op jit(solution)/shard_map/dipole_cg/pallas_call | solution.py:529
  69.9 0.6 copy.14
  70.5 0.6 copy.15
Async XLA Ops:
  0.6 0.7 copy-start.4
  0.6 0.7 copy-start.3
  1.3 0.8 %copy-start = (s32[112,128]{1,0:T(8,128)S(1)}, s32[112,128]{1,0:T(8,128)}, u32[]{:S(2)}) copy-start(s32[112,128]{1,0:T(8,128)} %constant.2.clone.keys) | copy-start | bytes 172036
  2.2 0.7 copy-start.1
  2.9 0.7 copy-start.2
  3.6 0.7 copy-start.5

commit v3 on v2

--- a/solution.py
+++ b/solution.py
@@ -97,10 +97,10 @@
     return parts[0:8] + parts[8:16]
 
 
-def kernel(sizes, pos, pol, fld, grp, prs, keys, dip_out, res_out,
-           hxyz, c3p, xi, mi, ms, mjp, f1, g1, f2own, g2own, flag, xj,
+def kernel(sizes, pos_in, pol_in, fld_in, grp_in, prs_in, keys_in, dip_out, res_out,
+           pos, pol, fld, grp, prs, keys, hxyz, c3p, xi, mi, ms, mjp, f1, g1, f2own, g2own, flag, xj,
            own, vec, polar8, send, halo, back, fold, ar_send, ar_recv,
-           hs_sem, hr_sem, fs_sem, fr_sem, as_sem, ar_sem):
+           in_sem, hs_sem, hr_sem, fs_sem, fr_sem, as_sem, ar_sem):
     f32, bf16 = jnp.float32, jnp.bfloat16
     me = tuple(lax.axis_index(a) for a in AXES)
     gx, gy, gz = me
@@ -117,6 +117,13 @@
         if phase == 1:
             return (lax.rem(gx + k, 8), gy, gz)
         return (gx, lax.rem(zed + k, 8) * 2 + core, gz)
+
+    arguments = (pos_in, pol_in, fld_in, grp_in, prs_in, keys_in)
+    taken = [
+        pltpu.make_async_copy(src, dst, in_sem.at[i])
+        for i, (src, dst) in enumerate(zip(arguments, (pos, pol, fld, grp, prs, keys)))]
+    for copy in taken:
+        copy.start()
 
     barrier = pltpu.get_barrier_semaphore()
     signals = 0
@@ -139,6 +146,9 @@
         rows = [jnp.sum(f, axis=0, keepdims=True) for f in sums]
         return put(*rows) - jnp.where(vec_rows, fold_parts(parts), 0.0)
 
+    for copy in taken:
+        copy.wait()
+
     for a in range(TILES):
         p = pol[a : a + 1]
         polar8[a] = jnp.broadcast_to(p * SCALE, (8, 128))
@@ -166,7 +176,7 @@
             send[r, slot] = own[r, SLOT_TILE[slot]]
         if r == 0:
             pl.semaphore_wait(barrier, signals)
-        for m in range(N_MSG):
+        for m in reversed(range(N_MSG)):
             halo_copy(r, m).start()
 
     send_halo(0)
@@ -273,18 +283,19 @@
 
     kinds = ((0, 3, 4, 0, face_list, 1), (3, 9, 2, 12, edge_list, 2), (9, 13, 1, 24, corner_list, 4))
 
-    def send_back(r):
-        for low, high, count, start, entries, group in kinds:
-            def one(step, carry):
-                for k in [step * group + u for u in range(group)]:
-                    fields = on_seconds(entries(k))
-                    for q in range(count):
-                        back[r, start + k * count + q] = tile_field(*fields[q])
-                return carry
-
-            lax.fori_loop(0, (high - low) // group, one, 0)
-            for m in range(low, high):
-                fold_copy(r, m).start()
+    def send_back(r, kind):
+        low, high, count, start, entries, group = kinds[kind]
+
+        def one(step, carry):
+            for k in [step * group + u for u in range(group)]:
+                fields = on_seconds(entries(k))
+                for q in range(count):
+                    back[r, start + k * count + q] = tile_field(*fields[q])
+            return carry
+
+        lax.fori_loop(0, (high - low) // group, one, 0)
+        for m in range(low, high):
+            fold_copy(r, m).start()
 
     def take_halo(r, kind):
         low, high, count, start, entries, group = kinds[kind]
@@ -299,50 +310,57 @@
 
         lax.fori_loop(0, (high - low) // group, one, 0)
 
-    def own_tiles(r):
-        f2own[...] = jnp.zeros_like(f2own)
-        g2own[...] = jnp.zeros_like(g2own)
-
+    def own_tiles(r, seconds, firsts):
         def near(a, carry):
             ns = [OWN + a * 4 + d for d in range(4)]
             bs = [lax.rem(a + d, 8) for d in range(4)]
-            tiles = [own[r, b] for b in bs]
-            mj = [triple(t) for t in tiles]
-            two = jnp.dot(ms[a], beside(ns), preferred_element_type=f32)
-            wide = jnp.concatenate([ms[b, :, 0:128] for b in bs[1:]], axis=1)
-            g1[a] = lax.dot_general(
-                wide, beside(ns[1:]), (((1,), (1,)), ((), ())), preferred_element_type=f32)
+            if seconds:
+                two = jnp.dot(ms[a], beside(ns), preferred_element_type=f32)
+            if firsts:
+                mj = [triple(own[r, b]) for b in bs]
+                wide = jnp.concatenate([ms[b, :, 0:128] for b in bs[1:]], axis=1)
+                g1[a] = lax.dot_general(
+                    wide, beside(ns[1:]), (((1,), (1,)), ((), ())), preferred_element_type=f32)
             sums = [[jnp.zeros((8, 128), f32)] * 3 for _ in range(4)]
             for g in range(16):
                 rows = slice(8 * g, 8 * g + 8)
                 m = [mi[a, rows, c * 128 : c * 128 + 128] for c in range(3)]
                 first = None
                 for d in range(4):
+                    if d == 0 and not seconds:
+                        continue
                     h = [hxyz[ns[d], c, rows, :] for c in range(3)]
-                    t = dot_rows(h, m)
-                    sums[d] = [sums[d][c] + h[c] * t for c in range(3)]
-                    if d > 0:
+                    if seconds:
+                        t = dot_rows(h, m)
+                        sums[d] = [sums[d][c] + h[c] * t for c in range(3)]
+                    if firsts and d > 0:
                         t = dot_rows(h, mj[d])
                         add = [h[c] * t for c in range(3)]
                         first = add if first is None else [first[c] + add[c] for c in range(3)]
-                for c in range(3):
-                    f1[a, c, rows, :] = first[c]
-            vec[r, a] = tile_field(sums[0], two[:, 0:128])
-            for d in range(1, 4):
-                for c in range(3):
-                    f2own[bs[d], c] += sums[d][c]
-                g2own[bs[d]] += two[:, d * 128 : d * 128 + 128]
+                if firsts:
+                    for c in range(3):
+                        f1[a, c, rows, :] = first[c]
+            if seconds:
+                vec[r, a] = tile_field(sums[0], two[:, 0:128])
+                for d in range(1, 4):
+                    for c in range(3):
+                        f2own[bs[d], c] += sums[d][c]
+                    g2own[bs[d]] += two[:, d * 128 : d * 128 + 128]
             return carry
 
+        if seconds:
+            f2own[...] = jnp.zeros_like(f2own)
+            g2own[...] = jnp.zeros_like(g2own)
         lax.fori_loop(0, TILES, near, 0)
-
         for a in range(4):
             entry = [(a, [LAST + a])]
-            fields, parts = on_seconds(entry)[0]
-            for c in range(3):
-                f2own[a + 4, c] += fields[c]
-            g2own[a + 4] += parts
-            on_firsts(entry, [own[r, a + 4]], ms[a + 4, :, 0:128])
+            if seconds:
+                fields, parts = on_seconds(entry)[0]
+                for c in range(3):
+                    f2own[a + 4, c] += fields[c]
+                g2own[a + 4] += parts
+            if firsts:
+                on_firsts(entry, [own[r, a + 4]], ms[a + 4, :, 0:128])
 
     def own_sums(r):
         total = jnp.zeros((8, 128), f32)
@@ -404,8 +422,6 @@
     lax.fori_loop(0, 8, own_near, 0)
     for a in range(4):
         coefficients(LAST + a, a, own[0, a + 4], True)
-    own_tiles(0)
-    own_sums(0)
     wait_halo(0)
     for e, start, count in MESSAGES:
         shift = jnp.where(row == 0, e[0] * BOX_EDGE, 0.0) + jnp.where(
@@ -425,11 +441,15 @@
                 coefficients(EDGE + k * 4 + p * 2 + q, edge_first(k, p), xj[12 + k * 2 + q], False)
         return carry
 
-    lax.fori_loop(0, 12, face_one, 0)
-    lax.fori_loop(0, 6, edge_one, 0)
     for k in range(4):
         coefficients(CORNER + k, corner_first(k), xj[24 + k], False)
-    send_back(0)
+    send_back(0, 2)
+    lax.fori_loop(0, 6, edge_one, 0)
+    send_back(0, 1)
+    lax.fori_loop(0, 12, face_one, 0)
+    send_back(0, 0)
+    own_tiles(0, True, True)
+    own_sums(0)
     for kind in range(3):
         take_halo(0, kind)
     first_sums(0)
@@ -440,8 +460,9 @@
             own[r, a] = polar8[a] * vec[r - 1, a]
         send_halo(r)
         columns(r)
-        send_back(r)
-        own_tiles(r)
+        for kind in (2, 1, 0):
+            send_back(r, kind)
+        own_tiles(r, True, r == 1)
         g12 = own_sums(r)
         wait_halo(r)
         if r == 2:
@@ -449,21 +470,23 @@
                 g12 = g12 + 2.0 * (halo[2, slot] * back[2, slot])
             parts = [
                 rows_dot(vec[0], own[1]), rows_dot(vec[1], own[1]), rows_dot(vec[1], own[2]), g12]
-            parts = [jnp.sum(g, axis=0, keepdims=True) for g in parts]
-            start_phase(0, jnp.where(row == 0, parts[0], jnp.where(
-                row == 1, parts[1], jnp.where(row == 2, parts[2], parts[3]))))
+            parts = [jnp.sum(jnp.sum(g, axis=0, keepdims=True), axis=1, keepdims=True) for g in parts]
+            lane = lax.broadcasted_iota(jnp.int32, (1, 128), 1)
+            start_phase(0, jnp.where(lane == 0, parts[0], jnp.where(
+                lane == 1, parts[1], jnp.where(lane == 2, parts[2], parts[3]))))
+            own_tiles(2, False, True)
         take_halo(r, 0)
         if r == 2:
             start_phase(1, end_phase(0))
         take_halo(r, 1)
         take_halo(r, 2)
+        first_sums(r)
         if r == 2:
             start_phase(2, end_phase(1))
-        first_sums(r)
         add_folded(r)
 
-    sums = jnp.sum(end_phase(2), axis=1, keepdims=True)
-    s00, s01, s11, s12 = (sums[i : i + 1] for i in range(4))
+    sums = end_phase(2)
+    s00, s01, s11, s12 = (sums[:, i : i + 1] for i in range(4))
     alpha = s00 / (s00 - s01)
     keep = 1.0 - alpha
     rho = keep * keep * s00 + 2.0 * keep * alpha * s01 + alpha * alpha * s11
@@ -497,8 +520,17 @@
 
     def shards(positions, polar, field, groups, pair_tiles):
         vmem = pl.BlockSpec(memory_space=pltpu.VMEM)
+        anywhere = pl.BlockSpec(memory_space=pl.ANY)
         dma = pltpu.SemaphoreType.DMA
+        atoms = positions.shape[-1]
+        rows = atoms // TILE
         scratch = [
+            pltpu.VMEM((3 * rows, TILE), f32),
+            pltpu.VMEM((rows, TILE), f32),
+            pltpu.VMEM((3 * rows, TILE), f32),
+            pltpu.VMEM((rows, TILE), jnp.int32),
+            pltpu.VMEM((3, 1, pair_tiles.shape[-1]), jnp.int32),
+            pltpu.VMEM((ENTRIES, 128), jnp.int32),
             pltpu.VMEM((ENTRIES, 3, 128, 128), f32),
             pltpu.VMEM((ENTRIES, 256, 128), bf16),
             pltpu.VMEM((8, 128, 640), f32),
@@ -518,22 +550,21 @@
             pltpu.VMEM((3, N_SLOTS, 8, 128), f32),
             pltpu.VMEM((3, N_SLOTS, 8, 128), f32),
             pltpu.VMEM((3, N_SLOTS, 8, 128), f32),
-            pltpu.VMEM((3, 8, 128), f32),
-            pltpu.VMEM((3, 7, 8, 128), f32),
+            pltpu.VMEM((3, 1, 128), f32),
+            pltpu.VMEM((3, 7, 1, 128), f32),
+            dma((6,)),
             dma((3, N_MSG)), dma((3, N_MSG)), dma((3, N_MSG)), dma((3, N_MSG)),
             dma((3, 7)), dma((3, 7)),
         ]
-        atoms = positions.shape[-1]
-        rows = atoms // TILE
         out = jax.ShapeDtypeStruct((3 * rows, TILE), f32)
         dip, res = pl.pallas_call(
             functools.partial(kernel, sizes),
             out_shape=(out, out),
-            in_specs=[vmem] * 6,
+            in_specs=[anywhere] * 6,
             out_specs=(vmem, vmem),
             scratch_shapes=scratch,
             compiler_params=pltpu.CompilerParams(
-                collective_id=0, has_side_effects=True, vmem_limit_bytes=50 * 1024 * 1024),
+                collective_id=0, has_side_effects=True, vmem_limit_bytes=64 * 1024 * 1024),
             name="dipole_cg",
         )(positions.reshape(3 * rows, TILE), polar.reshape(rows, TILE), field.reshape(3 * rows, TILE),
           groups.reshape(rows, TILE), pair_tiles.reshape(3, 1, -1), jnp.asarray(KEYS))

time: 71.8 us -> 67.2 us (0.936)
  local copies, waits for them, and re-layouts: 4.8 us -> 1.92 us
  Pallas kernels: 65.6 us -> 64.3 us
    unnamed x14 -> x4, local copies, waits for them, and re-layouts: 4.8 us -> 1.92 us
    pallas_call x1, Pallas kernels: 65.6 us -> 64.3 us  [shards(): pl.pallas_call(functools.partial(kernel, sizes), out_shape=(out, out), in...]
where the time goes in v3:
time: 67.2 us; the launch traced here: 66.9 us
  Pallas kernels  64.3 us (96%)
  local copies, waits for them, and re-layouts  1.92 us (3%)
    pallas_call x1, Pallas kernels, shards(): pl.pallas_call(functools.partial(kernel, sizes), out_shape=(out, out), in...  64.3 us
    unnamed x4, local copies, waits for them, and re-layouts  1.92 us

profile of v3, /device:TPU:1, one launch (start us, length us, event | category | flops | bytes accessed | tf_op | source)
XLA Modules:
  0.0 66.9 jit_solution(3668804186381664217)
XLA Ops:
  0.6 64.3 %dipole_cg.1 = (f32[24,128]{1,0:T(8,128)}, f32[24,128]{1,0:T(8,128)}) custom-call(f32[24,128]{1,0:T(8,128)} %bitcast.9, f32[8,128]{1,0:T(8,128)} %bitcast.11, f32[24,128]{1,0:T(8,128)} %bitcast.10, s32[8,128]{1,0:T(8,128)} %bitcast.12, s32[3,1,112]{2,1,0:T(1,128)} %bitcast.13, s32[112,128]{1,0:T(8,128)} %constant.2.clone.keys_in), custom_call_target="tpu_custom_call" | custom-call | tf_op jit(solution)/shard_map/dipole_cg/pallas_call | solution.py:560
  64.9 0.0 copy-start
  65.0 1.3 %copy.14 = f32[1,1,1,3,1024]{4,2,3,1,0:T(1,128)} copy(f32[1,1,1,3,1024]{4,2,3,1,0:T(1,128)} %bitcast.8) | data formatting | bytes 24576
  66.3 0.0 copy-done
  66.3 0.6 copy.15
Async XLA Ops:
  64.9 1.3 %copy-start = (f32[24,128]{1,0:T(8,128)S(1)}, f32[24,128]{1,0:T(8,128)}, u32[]{:S(2)}) copy-start(f32[24,128]{1,0:T(8,128)} %get-tuple-element.5) | copy-start | bytes 36868

commit v4 on v3

--- a/solution.py
+++ b/solution.py
@@ -97,7 +97,7 @@
     return parts[0:8] + parts[8:16]
 
 
-def kernel(sizes, pos_in, pol_in, fld_in, grp_in, prs_in, keys_in, dip_out, res_out,
+def kernel(sizes, pos_in, pol_in, fld_in, grp_in, prs_in, keys_in, out,
            pos, pol, fld, grp, prs, keys, hxyz, c3p, xi, mi, ms, mjp, f1, g1, f2own, g2own, flag, xj,
            own, vec, polar8, send, halo, back, fold, ar_send, ar_recv,
            in_sem, hs_sem, hr_sem, fs_sem, fr_sem, as_sem, ar_sem):
@@ -203,35 +203,36 @@
 
     def coefficients(n, a, tile, grouped):
         shift = flag[pl.ds(n, 1), :]
-        xs = [jnp.broadcast_to(tile[c : c + 1], (16, 128)) for c in range(4)]
-        xs[0] = xs[0] + jnp.broadcast_to(shift, (16, 128))
-        group = jnp.broadcast_to(tile[7:8], (16, 128))
-        for g in range(8):
-            rows = slice(16 * g, 16 * g + 16)
-            s = [xs[c] - xi[a, rows, c * 128 : c * 128 + 128] for c in range(3)]
-            r2 = s[0] * s[0] + s[1] * s[1] + s[2] * s[2]
-            if grouped:
-                r2 = jnp.where(xi[a, rows, 512:640] == group, FAR * FAR, r2)
-            rinv = lax.rsqrt(r2)
-            r = r2 * rinv
-            x = r2 * r * (xi[a, rows, 384:512] * xs[3])
-            ex = jnp.exp(x)
-            l3 = 1.0 - ex
-            v = jnp.clip(r - 8.0, -1.0, 1.0)
-            v2 = v * v
-            cut = jnp.maximum(C8 - v * ((v2 - C10) * v2 + 5.0), 0.0)
-            w = cut * (rinv * rinv * rinv)
-            c3 = w * l3
-            q2 = w * (l3 + x * ex)
-            q = q2 * lax.rsqrt(jnp.maximum(q2, 1e-36)) * rinv
-            for c in range(3):
-                hxyz[n, c, rows, :] = q * s[c]
-            hi = c3.astype(bf16)
-            c3p[n, rows, :] = hi
-            c3p[n, 128 + 16 * g : 144 + 16 * g, :] = (c3 - hi.astype(f32)).astype(bf16)
+        xs = [tile[c : c + 1] for c in range(4)]
+        xs[0] = xs[0] + shift
+        group = tile[7:8]
+        s = [xs[c] - xi[a, :, c * 128 : c * 128 + 128] for c in range(3)]
+        r2 = s[0] * s[0] + s[1] * s[1] + s[2] * s[2]
+        if grouped:
+            r2 = jnp.where(xi[a, :, 512:640] == group, FAR * FAR, r2)
+        rinv = lax.rsqrt(r2)
+        r = r2 * rinv
+        x = r2 * r * (xi[a, :, 384:512] * xs[3])
+        ex = jnp.exp(x)
+        l3 = 1.0 - ex
+        v = jnp.clip(r - 8.0, -1.0, 1.0)
+        v2 = v * v
+        cut = jnp.maximum(C8 - v * ((v2 - C10) * v2 + 5.0), 0.0)
+        w = cut * (rinv * rinv * rinv)
+        c3 = w * l3
+        q2 = w * (l3 + x * ex)
+        q = q2 * lax.rsqrt(jnp.maximum(q2, 1e-36)) * rinv
+        for c in range(3):
+            hxyz[n, c] = q * s[c]
+        hi = c3.astype(bf16)
+        c3p[n, 0:128] = hi
+        c3p[n, 128:256] = (c3 - hi.astype(f32)).astype(bf16)
 
     def beside(ns):
         return jnp.concatenate([c3p[n] for n in ns], axis=1) if len(ns) > 1 else c3p[ns[0]]
+
+    def by_eight(x):
+        return jnp.sum(x.reshape(4, 8, 128), axis=0)
 
     def dot_rows(h, m):
         return h[0] * m[0] + h[1] * m[1] + h[2] * m[2]
@@ -243,18 +244,18 @@
             part = jnp.dot(ms[a], beside(ns), preferred_element_type=f32)
             parts = part if parts is None else parts + part
         for a, ns in firsts:
-            for g in range(16):
-                rows = slice(8 * g, 8 * g + 8)
+            for g in range(4):
+                rows = slice(32 * g, 32 * g + 32)
                 m = [mi[a, rows, c * 128 : c * 128 + 128] for c in range(3)]
                 for q in range(count):
                     h = [hxyz[ns[q], c, rows, :] for c in range(3)]
                     d = dot_rows(h, m)
-                    add = [h[c] * d for c in range(3)]
+                    add = [by_eight(h[c] * d) for c in range(3)]
                     sums[q] = add if sums[q] is None else [sums[q][c] + add[c] for c in range(3)]
         return [(sums[q], parts[:, q * 128 : q * 128 + 128]) for q in range(count)]
 
     def triple(tile):
-        return [jnp.broadcast_to(tile[4 + c : 5 + c] * 3.0, (8, 128)) for c in range(3)]
+        return [tile[4 + c : 5 + c] * 3.0 for c in range(3)]
 
     def on_firsts(firsts, tiles, rows_of_parts):
         mj = [triple(t) for t in tiles]
@@ -262,8 +263,8 @@
             g1[a] += lax.dot_general(
                 rows_of_parts, beside(ns), (((1,), (1,)), ((), ())), preferred_element_type=f32)
         for a, ns in firsts:
-            for g in range(16):
-                rows = slice(8 * g, 8 * g + 8)
+            for g in range(4):
+                rows = slice(32 * g, 32 * g + 32)
                 sums = [f1[a, c, rows, :] for c in range(3)]
                 for q, n in enumerate(ns):
                     h = [hxyz[n, c, rows, :] for c in range(3)]
@@ -281,7 +282,7 @@
     def corner_list(k):
         return [(corner_first(k), [CORNER + k])]
 
-    kinds = ((0, 3, 4, 0, face_list, 1), (3, 9, 2, 12, edge_list, 2), (9, 13, 1, 24, corner_list, 4))
+    kinds = ((0, 3, 4, 0, face_list, 1), (3, 9, 2, 12, edge_list, 6), (9, 13, 1, 24, corner_list, 4))
 
     def send_back(r, kind):
         low, high, count, start, entries, group = kinds[kind]
@@ -311,7 +312,7 @@
         lax.fori_loop(0, (high - low) // group, one, 0)
 
     def own_tiles(r, seconds, firsts):
-        def near(a, carry):
+        def near(a):
             ns = [OWN + a * 4 + d for d in range(4)]
             bs = [lax.rem(a + d, 8) for d in range(4)]
             if seconds:
@@ -322,8 +323,8 @@
                 g1[a] = lax.dot_general(
                     wide, beside(ns[1:]), (((1,), (1,)), ((), ())), preferred_element_type=f32)
             sums = [[jnp.zeros((8, 128), f32)] * 3 for _ in range(4)]
-            for g in range(16):
-                rows = slice(8 * g, 8 * g + 8)
+            for g in range(4):
+                rows = slice(32 * g, 32 * g + 32)
                 m = [mi[a, rows, c * 128 : c * 128 + 128] for c in range(3)]
                 first = None
                 for d in range(4):
@@ -332,7 +333,7 @@
                     h = [hxyz[ns[d], c, rows, :] for c in range(3)]
                     if seconds:
                         t = dot_rows(h, m)
-                        sums[d] = [sums[d][c] + h[c] * t for c in range(3)]
+                        sums[d] = [sums[d][c] + by_eight(h[c] * t) for c in range(3)]
                     if firsts and d > 0:
                         t = dot_rows(h, mj[d])
                         add = [h[c] * t for c in range(3)]
@@ -346,12 +347,16 @@
                     for c in range(3):
                         f2own[bs[d], c] += sums[d][c]
                     g2own[bs[d]] += two[:, d * 128 : d * 128 + 128]
+
+        def pair(k, carry):
+            near(2 * k)
+            near(2 * k + 1)
             return carry
 
         if seconds:
             f2own[...] = jnp.zeros_like(f2own)
             g2own[...] = jnp.zeros_like(g2own)
-        lax.fori_loop(0, TILES, near, 0)
+        lax.fori_loop(0, TILES // 2, pair, 0)
         for a in range(4):
             entry = [(a, [LAST + a])]
             if seconds:
@@ -502,8 +507,8 @@
         dip = d0 * own[0, a] + d1 * own[1, a] + d2 * own[2, a]
         res = r0 * vec[0, a] + r1 * vec[1, a] + r2 * vec[2, a]
         for c in range(3):
-            dip_out[8 * c + a : 8 * c + a + 1] = dip[4 + c : 5 + c]
-            res_out[8 * c + a : 8 * c + a + 1] = res[4 + c : 5 + c]
+            out[0, 8 * c + a : 8 * c + a + 1] = dip[4 + c : 5 + c]
+            out[1, 8 * c + a : 8 * c + a + 1] = res[4 + c : 5 + c]
 
     for r in range(3):
         for m in range(N_MSG):
@@ -556,19 +561,18 @@
             dma((3, N_MSG)), dma((3, N_MSG)), dma((3, N_MSG)), dma((3, N_MSG)),
             dma((3, 7)), dma((3, 7)),
         ]
-        out = jax.ShapeDtypeStruct((3 * rows, TILE), f32)
-        dip, res = pl.pallas_call(
+        out = pl.pallas_call(
             functools.partial(kernel, sizes),
-            out_shape=(out, out),
+            out_shape=jax.ShapeDtypeStruct((2, 3 * rows, TILE), f32),
             in_specs=[anywhere] * 6,
-            out_specs=(vmem, vmem),
+            out_specs=vmem,
             scratch_shapes=scratch,
             compiler_params=pltpu.CompilerParams(
                 collective_id=0, has_side_effects=True, vmem_limit_bytes=64 * 1024 * 1024),
             name="dipole_cg",
         )(positions.reshape(3 * rows, TILE), polar.reshape(rows, TILE), field.reshape(3 * rows, TILE),
           groups.reshape(rows, TILE), pair_tiles.reshape(3, 1, -1), jnp.asarray(KEYS))
-        return dip.reshape(1, 1, 1, 3, atoms), res.reshape(1, 1, 1, 3, atoms)
+        return out[0].reshape(1, 1, 1, 3, atoms), out[1].reshape(1, 1, 1, 3, atoms)
 
     placed = (
         P(*AXES, None, None), P(*AXES, None), P(*AXES, None, None), P(*AXES, None), P(*AXES, None, None))

time: 67.2 us -> 64.6 us (0.961)
  Pallas kernels: 64.3 us -> 62.4 us
    pallas_call x1, Pallas kernels: 64.3 us -> 62.4 us  [shards(): pl.pallas_call(functools.partial(kernel, sizes), out_shape=jax.ShapeDtype...]
    unnamed x4 -> x0, local copies, waits for them, and re-layouts: 1.92 us -> none
    slice x0 -> x1, local copies, waits for them, and re-layouts: none -> 1.33 us  [shards(): out[1].reshape(1, 1, 1, 3, atoms)]
where the time goes in v4:
time: 64.6 us; the launch traced here: 64.3 us
  Pallas kernels  62.4 us (97%)
  local copies, waits for them, and re-layouts  1.33 us (2%)
    pallas_call x1, Pallas kernels, shards(): pl.pallas_call(functools.partial(kernel, sizes), out_shape=jax.ShapeDtype...  62.4 us
    slice x1, local copies, waits for them, and re-layouts, shards(): out[1].reshape(1, 1, 1, 3, atoms)  1.33 us

profile of v4, /device:TPU:1, one launch (start us, length us, event | category | flops | bytes accessed | tf_op | source)
XLA Modules:
  0.0 64.3 jit_solution(4841061567785167898)
XLA Ops:
  0.6 62.4 %dipole_cg.1 = f32[2,24,128]{2,1,0:T(8,128)} custom-call(f32[24,128]{1,0:T(8,128)} %bitcast.7, f32[8,128]{1,0:T(8,128)} %bitcast.11, f32[24,128]{1,0:T(8,128)} %bitcast.8, s32[8,128]{1,0:T(8,128)} %bitcast.12, s32[3,1,112]{2,1,0:T(1,128)} %bitcast.13, s32[112,128]{1,0:T(8,128)} %constant.2.clone.keys_in), custom_call_target="tpu_custom_call" | custom-call | tf_op jit(solution)/shard_map/dipole_cg/pallas_call | solution.py:564
  63.0 1.3 %fusion = (f32[1,24,128]{2,1,0:T(8,128)}, f32[1,24,128]{2,1,0:T(8,128)}) fusion(f32[2,24,128]{2,1,0:T(8,128)} %dipole_cg.1), kind=kLoop, calls=%fused_computation | loop fusion | bytes 49152 | tf_op jit(solution)/shard_map/slice | solution.py:575

commit v5 on v4

--- a/solution.py
+++ b/solution.py
@@ -401,7 +401,7 @@
 
     def start_phase(phase, total):
         ar_send[phase] = total
-        for k in range(1, 8):
+        for k in (4, 3, 5, 2, 6, 1, 7):
             phase_copy(phase, k).start()
 
     def end_phase(phase):
@@ -480,11 +480,11 @@
             start_phase(0, jnp.where(lane == 0, parts[0], jnp.where(
                 lane == 1, parts[1], jnp.where(lane == 2, parts[2], parts[3]))))
             own_tiles(2, False, True)
-        take_halo(r, 0)
+        take_halo(r, 1)
+        take_halo(r, 2)
         if r == 2:
             start_phase(1, end_phase(0))
-        take_halo(r, 1)
-        take_halo(r, 2)
+        take_halo(r, 0)
         first_sums(r)
         if r == 2:
             start_phase(2, end_phase(1))

time: 64.6 us -> 65.2 us (level)
  no operation moved by 1% of the time
where the time goes in v5:
time: 65.2 us; the launch traced here: 64.9 us
  Pallas kernels  63 us (97%)
  local copies, waits for them, and re-layouts  1.33 us (2%)
    pallas_call x1, Pallas kernels, shards(): pl.pallas_call(functools.partial(kernel, sizes), out_shape=jax.ShapeDtype...  63 us
    slice x1, local copies, waits for them, and re-layouts, shards(): out[1].reshape(1, 1, 1, 3, atoms)  1.33 us

profile of v5, /device:TPU:1, one launch (start us, length us, event | category | flops | bytes accessed | tf_op | source)
XLA Modules:
  0.0 64.9 jit_solution(3135332954862931950)
XLA Ops:
  0.6 63.0 %dipole_cg.1 = f32[2,24,128]{2,1,0:T(8,128)} custom-call(f32[24,128]{1,0:T(8,128)} %bitcast.7, f32[8,128]{1,0:T(8,128)} %bitcast.11, f32[24,128]{1,0:T(8,128)} %bitcast.8, s32[8,128]{1,0:T(8,128)} %bitcast.12, s32[3,1,112]{2,1,0:T(1,128)} %bitcast.13, s32[112,128]{1,0:T(8,128)} %constant.2.clone.keys_in), custom_call_target="tpu_custom_call" | custom-call | tf_op jit(solution)/shard_map/dipole_cg/pallas_call | solution.py:564
  63.6 1.3 %fusion = (f32[1,24,128]{2,1,0:T(8,128)}, f32[1,24,128]{2,1,0:T(8,128)}) fusion(f32[2,24,128]{2,1,0:T(8,128)} %dipole_cg.1), kind=kLoop, calls=%fused_computation | loop fusion | bytes 49152 | tf_op jit(solution)/shard_map/slice | solution.py:575
